TPU v7x, 32 devices: a whole 2x2x4 slice. The times are simulated.
32 devices in a mesh: seq: 8 (over z, x), feat: 4 (over y, core).
Axes of the slice: x: 2, y: 2, z: 4, core: 2. Of those that a mesh axis runs over, the one named last changes fastest.
Arguments:
- tokens: bfloat16 [4096, 8192], P('seq', 'feat'), may hold values from -6 to 6
- butterfly: bfloat16 [16, 5, 512, 896], P('feat'), may hold values from -0.125 to 0.125
- low_in: bfloat16 [8192, 256], P('feat'), may hold values from -0.0625 to 0.0625
- low_out: bfloat16 [256, 14336], P(None, 'feat'), may hold values from -0.375 to 0.375
- cotangent: bfloat16 [4096, 14336], P('seq', 'feat'), may hold values from -6 to 6
Outputs:
- activated: bfloat16 [4096, 14336], P('seq', 'feat')
- tokens_grad: bfloat16 [4096, 8192], P('seq', 'feat')
- butterfly_grad: float32 [16, 5, 512, 896], P('feat', None, 'seq')
- low_in_grad: float32 [8192, 256], P('feat', 'seq')
- low_out_grad: float32 [256, 14336], P('seq', 'feat')
All inputs are finite; a program needn't handle non-finite values.
Results may differ from a plain program's by a relative error of at most 0.0058.
Values may be sent and summed in bfloat16 or wider, within the bound.
A program may use at most 192 MiB of HBM per device.

v0:
```python
import jax
import jax.numpy as jnp
import numpy as np
from jax import lax
from jax.sharding import PartitionSpec as P


def from_partner(block, axis, bit):
    count = lax.axis_size(axis)
    route = []
    for low in range(count):
        high = low | 1 << bit
        if high != low and high < count:
            route += [(low, high), (high, low)]
    return lax.ppermute(block, axis, route)


def gelu_tanh(values):
    return jax.nn.gelu(values, approximate=True)


def local(tokens, butterfly, low_in, low_out, cotangent):
    count_rows = tokens.shape[0]
    per_dev = butterfly.shape[0]
    block_width = butterfly.shape[2]
    hidden_width = butterfly.shape[3]
    local_bits = per_dev.bit_length() - 1
    total_blocks = per_dev * lax.axis_size("feat")
    levels = total_blocks.bit_length() - 1
    own_blocks = tokens.reshape(count_rows, per_dev, block_width)
    partners = []
    gathered = lax.all_gather(tokens, "feat", axis=1, tiled=True)
    gathered = gathered.reshape(count_rows, total_blocks, block_width)
    first_block = lax.axis_index("feat") * per_dev
    for bit_level in range(levels):
        picks = jnp.bitwise_xor(first_block + jnp.arange(per_dev, dtype=jnp.int32), 1 << bit_level)
        partners.append(jnp.take(gathered, picks, axis=1))
    stacked = jnp.stack([own_blocks] + partners, axis=0)
    low_part = jnp.dot(tokens, low_in, preferred_element_type=jnp.float32)
    low_rank = lax.psum(low_part, "feat").astype(jnp.bfloat16)
    pre = jnp.einsum("stkc,ksch->tkh", stacked, butterfly, preferred_element_type=jnp.float32)
    pre = pre.reshape(count_rows, per_dev * hidden_width) + jnp.dot(
        low_rank, low_out, preferred_element_type=jnp.float32
    )
    activ, pullback = jax.vjp(gelu_tanh, pre)
    activated = activ.astype(jnp.bfloat16)
    grad_pre = pullback(cotangent.astype(jnp.float32))[0].astype(jnp.bfloat16)
    low_back = jnp.dot(grad_pre, low_out.T, preferred_element_type=jnp.float32)
    low_grad = lax.psum(low_back, "feat").astype(jnp.bfloat16)
    grad_blocks = grad_pre.reshape(count_rows, per_dev, hidden_width)
    input_grad = jnp.einsum(
        "tkh,kch->tkc", grad_blocks, butterfly[:, 0], preferred_element_type=jnp.float32
    )
    partials = jnp.einsum(
        "tkh,ksch->stkc", grad_blocks, butterfly[:, 1:], preferred_element_type=jnp.float32
    )
    for bit_level in range(levels):
        partial_value = partials[bit_level]
        if 1 << bit_level < per_dev:
            swapped_order = np.arange(per_dev) ^ 1 << bit_level
            input_grad = input_grad + partial_value[:, swapped_order]
        else:
            input_grad = input_grad + from_partner(partial_value, "feat", bit_level - local_bits)
    low_term = jnp.dot(low_grad, low_in.T, preferred_element_type=jnp.float32)
    tokens_grad = (input_grad.reshape(count_rows, per_dev * block_width) + low_term).astype(
        jnp.bfloat16
    )
    weight_terms = jnp.einsum(
        "stkc,tkh->ksch", stacked, grad_blocks, preferred_element_type=jnp.float32
    )
    in_terms = jnp.dot(tokens.T, low_grad, preferred_element_type=jnp.float32)
    out_terms = jnp.dot(low_rank.T, grad_pre, preferred_element_type=jnp.float32)
    butterfly_grad, low_in_grad, low_out_grad = (
        lax.psum_scatter(weight_terms, "seq", scatter_dimension=2, tiled=True),
        lax.psum_scatter(in_terms, "seq", scatter_dimension=1, tiled=True),
        lax.psum_scatter(out_terms, "seq", scatter_dimension=0, tiled=True),
    )
    return (activated, tokens_grad, butterfly_grad, low_in_grad, low_out_grad)


def solution(mesh):
    placed = (
        P("seq", "feat"),
        P("feat", None, None, None),
        P("feat", None),
        P(None, "feat"),
        P("seq", "feat"),
    )
    return jax.shard_map(
        local,
        mesh=mesh,
        in_specs=placed,
        out_specs=(
            P("seq", "feat"),
            P("seq", "feat"),
            P("feat", None, "seq", None),
            P("feat", "seq"),
            P("seq", "feat"),
        ),
        check_vma=False,
    )
```

profile of v0, /device:TPU:16, one launch (start us, length us, event | category | flops | bytes accessed | tf_op | source)
XLA Modules:
  0.0 946.0 jit_solution(3417779382372884852)
XLA Ops:
  7.2 0.0 copy-start
  7.2 0.0 all-gather.2.cloned.1.call-start
  7.2 4.0 copy.32
  11.3 0.0 copy-start.7
  11.3 0.0 all-gather.2.cloned.1.call-update
  11.3 0.0 reduce-scatter.6.cloned.1.call-start
  11.4 4.2 copy.38
  15.6 0.0 copy-done.7
  15.6 3.1 fusion.34
  18.8 3.3 constant_dynamic-update-slice_fusion
  22.1 26.8 %all-reduce.2 = bf16[512,256]{1,0:T(8,128)(2,1)S(1)} all-reduce(f32[512,256]{1,0:T(8,128)} %fusion.34), channel_id=1, replica_groups=mesh['seq'=8,'feat'=4] {'feat'}, use_global_device_ids=true, to_apply=%region_0.0 | all-reduce | flops 131072 | bytes 786432 | tf_op jit(solution)/shard_map/psum | solution.py:40
  48.9 30.3 %all-gather.2.cloned.1.call-done = bf16[512,8192]{0,1:T(8,128)(2,1)} async-done(((bf16[512,2048]{0,1:T(8,128)(2,1)}), bf16[512,8192]{0,1:T(8,128)(2,1)}) %all-gather.2.cloned.1.call-update) | async-done | bytes 8388624 | tf_op jit(solution)/shard_map/all_gather | solution.py:32
  79.2 12.3 %copy.34 = bf16[512,16,512]{2,0,1:T(8,128)(2,1)} copy(bf16[512,16,512]{0,2,1:T(8,128)(2,1)} %bitcast.80) | data formatting | bytes 16777216 | tf_op jit(solution)/shard_map/reshape | solution.py:33
  91.5 5.4 gather_fusion.2
  96.9 5.4 gather_fusion.3
  102.3 5.4 gather_fusion.4
  107.7 5.4 gather_fusion.5
  113.1 0.0 copy-start.6
  113.1 0.0 copy-start.5
  113.1 3.7 bitcast_dynamic-update-slice_fusion.3
  116.8 0.0 copy-done.6
  116.8 0.0 copy-start.4
  116.8 2.0 bitcast_dynamic-update-slice_fusion.2
  118.8 0.0 copy-done.5
  118.8 2.0 bitcast_dynamic-update-slice_fusion.1
  120.8 0.0 copy-done.4
  120.8 2.0 bitcast_dynamic-update-slice_fusion
  122.8 20.8 %convolution_bitcast_fusion = f32[512,4,896]{2,0,1:T(8,128)} fusion(bf16[5,512,4,512]{3,1,0,2:T(8,128)(2,1)} %bitcast_dynamic-update-slice_fusion, bf16[4,5,512,896]{3,2,1,0:T(8,128)(2,1)} %param.12), kind=kOutput, calls=%fused_computation.41 | convolution fusion | flops 9395240960 | bytes 36175872 | tf_op jit(solution)/shard_map/stkc,ksch->tkh/dot_general | solution.py:41
  143.6 7.9 copy.39
  151.5 8.4 copy.40
  159.9 0.0 copy-done
  159.9 10.3 %fusion.7 = (bf16[512,3584]{1,0:T(8,128)(2,1)S(1)}, bf16[512,3584]{1,0:T(8,128)(2,1)}) fusion(bf16[512,3584]{1,0:T(8,128)(2,1)} %param.15, f32[512,3584]{1,0:T(8,128)} %copy.40, bf16[512,256]{1,0:T(8,128)(2,1)S(1)} %all-reduce.2, bf16[256,3584]{1,0:T(8,128)(2,1)S(1)} %copy-done), kind=kOutput, calls=%fused_computation.15 | convolution fusion | flops 983564288 | bytes 20447232 | tf_op jit(solution)/shard_map/dot_general | solution.py:42
  170.2 0.0 copy-start.2
  170.2 1.8 copy-done.2
  172.0 1.9 fusion.35
  174.0 16.9 %all-reduce.3 = bf16[512,256]{1,0:T(8,128)(2,1)S(1)} all-reduce(f32[512,256]{1,0:T(8,128)} %fusion.35), channel_id=1, replica_groups=mesh['seq'=8,'feat'=4] {'feat'}, use_global_device_ids=true, to_apply=%region_1.3 | all-reduce | flops 131072 | bytes 786432 | tf_op jit(solution)/shard_map/psum | solution.py:49
  190.8 3.7 convolution_bitcast_fusion.1
  194.5 0.0 reduce-scatter.6.cloned.1.call-update
  194.5 0.0 reduce-scatter.8.cloned.1.call-start
  194.6 5.1 fusion.37
  199.7 0.0 reduce-scatter.8.cloned.1.call-update
  199.7 0.0 reduce-scatter.4.cloned.1.call-start
  199.7 7.3 reshape.29
  207.0 20.3 %fusion.19 = f32[4,5,512,896]{3,2,1,0:T(8,128)} fusion(bf16[5,512,4,512]{3,1,0,2:T(8,128)(2,1)} %bitcast_dynamic-update-slice_fusion, bf16[512,4,896,1]{2,1,0,3:T(4,128)(2,1)} %bitcast.81), kind=kOutput, calls=%fused_computation.36 | convolution fusion | flops 9395240960 | bytes 50855936 | tf_op jit(solution)/shard_map/stkc,tkh->ksch/dot_general | solution.py:68
  227.4 0.0 reduce-scatter.4.cloned.1.call-update
  227.4 16.6 %fusion.2 = f32[4,512,4,512]{1,3,2,0:T(8,128)} fusion(bf16[64,4,8,896]{3,2,1,0:T(8,128)(2,1)} %bitcast.75, bf16[4,5,512,896]{3,2,1,0:T(8,128)(2,1)} %param.12), kind=kOutput, calls=%fused_computation.12 | convolution fusion | flops 7516192768 | bytes 35127296 | tf_op jit(solution)/shard_map/tkh,ksch->stkc/dot_general | solution.py:54
  244.0 0.0 copy-start.9
  244.0 12.4 %slice_bitcast_fusion.3 = (f32[512,4,512]{0,2,1:T(8,128)}, f32[512,4,512]{0,2,1:T(8,128)}, f32[512,4,512]{0,2,1:T(8,128)}, f32[512,4,512]{0,2,1:T(8,128)}) fusion(f32[4,512,4,512]{1,3,2,0:T(8,128)} %fusion.2), kind=kLoop, calls=%fused_computation.28 | loop fusion | bytes 33554432 | tf_op jit(solution)/shard_map/squeeze | solution.py:58
  256.4 0.2 collective-permute-start
  256.7 1.1 collective-permute-start.1
  257.7 0.0 copy-done.8
  257.7 0.0 copy-done.9
  257.8 5.0 gather_fusion
  262.8 5.0 gather_fusion.1
  267.8 2.7 fusion.36
  270.5 0.0 collective-permute-done
  270.5 79.3 %collective-permute-done.1 = f32[512,4,512]{0,2,1:T(8,128)} collective-permute-done((f32[512,4,512]{0,2,1:T(8,128)}, f32[512,4,512]{0,2,1:T(8,128)}, u32[]{:S(2)}, u32[]{:S(2)}) %collective-permute-start.1) | collective-permute-done | bytes 4194336 | tf_op jit(solution)/shard_map/ppermute | solution.py:15
  349.7 0.0 copy-done.3
  349.7 11.6 %fusion.15 = f32[512,4,512]{0,2,1:T(8,128)} fusion(f32[512,4,512]{0,2,1:T(8,128)} %collective-permute-done.1, f32[512,4,512]{0,2,1:T(8,128)} %collective-permute-done, f32[4,512,512]{1,2,0:T(8,128)} %gather_fusion.1, f32[4,512,512]{1,2,0:T(8,128)} %gather_fusion, bf16[4,5,512,896]{3,2,1,0:T(8,128)(2,1)} %param.12, bf16[64,4,8,896]{3,2,1,0:T(8,128)(2,1)S(1)} %bitcast.76), kind=kOutput, calls=%fused_computation.30 | convolution fusion | flops 1883242496 | bytes 28311552 | tf_op jit(solution)/shard_map/tkh,kch->tkc/dot_general | solution.py:51
  361.3 5.5 copy.45
  366.8 5.5 add_convert_fusion
  372.3 0.0 reduce-scatter.6.cloned.1.call-done
  372.3 567.1 %reduce-scatter.4.cloned.1.call-done = f32[4,5,64,896]{3,2,1,0:T(8,128)} async-done(((f32[4,5,512,896]{3,2,1,0:T(8,128)}), f32[4,5,64,896]{3,2,1,0:T(8,128)}) %reduce-scatter.4.cloned.1.call-update) | async-done | bytes 4587536 | tf_op jit(solution)/shard_map/reduce_scatter | solution.py:74
  939.4 0.0 copy-done.1
  (14 shorter events, 0.1 us)
Async XLA Ops:
  7.2 152.8 %copy-start = (bf16[256,3584]{1,0:T(8,128)(2,1)S(1)}, bf16[256,3584]{1,0:T(8,128)(2,1)}, u32[]{:S(2)}) copy-start(bf16[256,3584]{1,0:T(8,128)(2,1)} %param.14) | copy-start | bytes 5505028
  7.2 72.1 %all-gather.2.cloned.1.call-start = ((), (), s32[]{:S(2)}) async-start(), calls=%async_computation.3 | async-start | bytes 10485760 | tf_op jit(solution)/shard_map/all_gather | solution.py:32
  11.3 4.3 copy-start.7
  11.3 361.0 %reduce-scatter.6.cloned.1.call-start = ((), (), s32[]{:S(2)}) async-start(), calls=%async_computation.5 | async-start | bytes 2359296 | tf_op jit(solution)/shard_map/reduce_scatter | solution.py:75
  113.1 3.7 copy-start.6
  113.1 5.7 copy-start.5
  116.8 4.0 copy-start.4
  170.2 1.8 copy-start.2
  194.5 177.7 %reduce-scatter.8.cloned.1.call-start = ((), (), s32[]{:S(2)}) async-start(), calls=%async_computation.6 | async-start | bytes 4128768 | tf_op jit(solution)/shard_map/reduce_scatter | solution.py:76
  199.7 739.8 %reduce-scatter.4.cloned.1.call-start = ((), (), s32[]{:S(2)}) async-start(), calls=%async_computation.4 | async-start | bytes 41287680 | tf_op jit(solution)/shard_map/reduce_scatter | solution.py:74
  244.0 13.7 %copy-start.8 = (s32[4]{0:T(128)S(1)}, s32[4]{0:T(128)}, u32[]{:S(2)}) copy-start(s32[4]{0:T(128)} %constant.46) | copy-start | bytes 52
  244.0 13.7 %copy-start.9 = (s32[4]{0:T(128)S(1)}, s32[4]{0:T(128)}, u32[]{:S(2)}) copy-start(s32[4]{0:T(128)} %constant.47) | copy-start | bytes 52
  256.4 14.0 %collective-permute-start = (f32[512,4,512]{0,2,1:T(8,128)}, f32[512,4,512]{0,2,1:T(8,128)}, u32[]{:S(2)}, u32[]{:S(2)}) collective-permute-start(f32[512,4,512]{0,2,1:T(8,128)} %get-tuple-element.8), channel_id=1, source_target_pairs={{0,1},{1,0},{2,3},{3,2},{4,5},{5,4},{6,7},{7,6},{8,9},{9,8},{10,11... | collective-permute-start | bytes 12582920 | tf_op jit(solution)/shard_map/ppermute | solution.py:15
  256.7 93.1 %collective-permute-start.1 = (f32[512,4,512]{0,2,1:T(8,128)}, f32[512,4,512]{0,2,1:T(8,128)}, u32[]{:S(2)}, u32[]{:S(2)}) collective-permute-start(f32[512,4,512]{0,2,1:T(8,128)} %get-tuple-element.7), channel_id=1, source_target_pairs={{0,2},{2,0},{1,3},{3,1},{4,6},{6,4},{5,7},{7,5},{8,10},{10,8},{9,1... | collective-permute-start | bytes 12582920 | tf_op jit(solution)/shard_map/ppermute | solution.py:15
  267.8 82.0 %copy-start.3 = (bf16[512,3584]{1,0:T(8,128)(2,1)S(1)}, bf16[512,3584]{1,0:T(8,128)(2,1)}, u32[]{:S(2)}) copy-start(bf16[512,3584]{1,0:T(8,128)(2,1)} %copy-done.2) | copy-start | bytes 11010052
  361.3 578.1 %copy-start.1 = (bf16[256,3584]{1,0:T(8,128)(2,1)S(1)}, bf16[256,3584]{1,0:T(8,128)(2,1)}, u32[]{:S(2)}) copy-start(bf16[256,3584]{1,0:T(8,128)(2,1)} %param.14) | copy-start | bytes 5505028
Sparse Core Ops, SparseCore 0:
  11.4 67.7 all-gather.1
  194.7 67.3 reduce-scatter.5
  266.3 80.5 reduce-scatter.7
  351.3 588.1 reduce-scatter.3
where the time goes:
time: 950 us; the launch traced here: 946 us
  waiting for transfers between devices  677 us (71%)
  local copies, waits for them, and re-layouts  98.8 us (10%)
  matrix products  96 us (10%)
  blocking collectives  43.7 us (5%)
  other arithmetic  15.3 us (2%)
  between operations  13.9 us (1%)
    reduce_scatter x1, waiting for transfers between devices, local(): lax.psum_scatter(weight_terms, 'seq', scatter_dimension=2, tiled=True)  567 us
    ppermute x2, waiting for transfers between devices, from_partner(): return lax.ppermute(block, axis, route)  79.3 us
    all_gather x1, waiting for transfers between devices, local(): gathered = lax.all_gather(tokens, 'feat', axis=1, tiled=True)  30.3 us
    psum x1, blocking collectives, local(): low_rank = lax.psum(low_part, 'feat').astype(jnp.bfloat16)  26.8 us
    gather x4, local copies, waits for them, and re-layouts, local(): partners.append(jnp.take(gathered, picks, axis=1))  21.5 us
    dot_general x1, matrix products, local(): jnp.einsum('stkc,ksch->tkh', stacked, butterfly, preferred_element_type=j...  20.8 us
    dot_general x1, matrix products, local(): jnp.einsum('stkc,tkh->ksch', stacked, grad_blocks, preferred_element_type...  20.3 us
  transfers between devices with their start and end apart: 6, of which 3 were waited for; matrix products, arithmetic and copies ran while one was open for 11% of the time, Pallas kernels for 0%

commit v1 on v0

v1 whole, which is shorter than its diff:
```python
import functools

import jax
import jax.numpy as jnp
from jax import lax
from jax.experimental import pallas as pl
from jax.experimental.pallas import tpu as pltpu
from jax.sharding import PartitionSpec as P

F32 = jnp.float32
BF16 = jnp.bfloat16


def swap(block, axis, distance):
    count = lax.axis_size(axis)
    return lax.ppermute(block, axis, [(i, i ^ distance) for i in range(count)])


def sum_over(part, axis):
    distance = 1
    while distance < lax.axis_size(axis):
        part = part + swap(part, axis, distance)
        distance *= 2
    return part


def line_scatter(parts, place, count):
    def pick(at):
        return lax.dynamic_index_in_dim(parts, jnp.clip(at, 0, count - 1), 0, keepdims=False)

    total = pick(place).astype(F32)
    for way in (1, -1):
        moving = None
        for step in range(1, count):
            term = pick(place + way * (count - step))
            if moving is not None:
                term = (term.astype(F32) + moving.astype(F32)).astype(BF16)
            froms = range(step) if way == 1 else range(count - step, count)
            route = [(2 * z + x, 2 * (z + way) + x) for z in froms for x in range(2)]
            moving = lax.ppermute(term, "seq", route)
        if moving is not None:
            total = total + moving.astype(F32)
    return total


def forward_body(slots, tile, *refs):
    sources = refs[:slots]
    low_rank, weights, low_out, cotangent, activated, grad_pre = refs[slots:]
    gain = 0.7978845608028654
    rows = low_rank.shape[0]
    for top in range(0, rows, tile):
        at = pl.ds(top, tile)
        value = jnp.dot(low_rank[at, :], low_out[...], preferred_element_type=F32)
        for slot in range(slots):
            value += jnp.dot(sources[slot][at, :], weights[0, slot], preferred_element_type=F32)
        square = value * value
        bend = jnp.tanh(gain * value * (1.0 + 0.044715 * square))
        half = 0.5 * (1.0 + bend)
        activated[at, :] = (value * half).astype(BF16)
        slope = half + 0.5 * gain * value * (1.0 - bend * bend) * (1.0 + 3 * 0.044715 * square)
        grad_pre[0, at, :] = (cotangent[at, :].astype(F32) * slope).astype(BF16)


def forward(tokens, partners, low_rank, butterfly, low_out, cotangent):
    rows = tokens.shape[0]
    per_dev, slots, block, hidden = butterfly.shape
    rank = low_out.shape[0]
    local_bits = per_dev.bit_length() - 1
    tile = 256 if rows % 256 == 0 else rows

    def column(distance):
        return pl.BlockSpec((rows, block), lambda k: (0, k ^ distance))

    arrays = [tokens] * (1 + local_bits) + partners
    specs = [column(0)] + [column(1 << b) for b in range(local_bits)] + [column(0)] * len(partners)
    wide = pl.BlockSpec((rows, hidden), lambda k: (0, k))
    return pl.pallas_call(
        functools.partial(forward_body, slots, tile),
        grid=(per_dev,),
        in_specs=specs
        + [
            pl.BlockSpec((rows, rank), lambda k: (0, 0)),
            pl.BlockSpec((1, slots, block, hidden), lambda k: (k, 0, 0, 0)),
            pl.BlockSpec((rank, hidden), lambda k: (0, k)),
            wide,
        ],
        out_specs=[wide, pl.BlockSpec((1, rows, hidden), lambda k: (k, 0, 0))],
        out_shape=[
            jax.ShapeDtypeStruct((rows, per_dev * hidden), BF16),
            jax.ShapeDtypeStruct((per_dev, rows, hidden), BF16),
        ],
        compiler_params=pltpu.CompilerParams(vmem_limit_bytes=48 << 20),
        cost_estimate=pl.CostEstimate(
            flops=2 * rows * per_dev * hidden * (slots * block + rank),
            bytes_accessed=2 * (butterfly.size + 3 * cotangent.size + slots * tokens.size),
            transcendentals=cotangent.size,
        ),
    )(*arrays, low_rank, butterfly, low_out, cotangent)


def dot_t(left, right):
    return lax.dot_general(left, right, (((1,), (1,)), ((), ())), preferred_element_type=F32)


def local(tokens, butterfly, low_in, low_out, cotangent):
    rows = tokens.shape[0]
    per_dev, slots, block, hidden = butterfly.shape
    rank = low_out.shape[0]
    seq = lax.axis_size("seq")
    feat = lax.axis_size("feat")
    local_bits = per_dev.bit_length() - 1
    remote = slots - 1 - local_bits
    pairs = seq // 2
    me = lax.axis_index("seq")
    side = me % 2
    place = me // 2
    width = block // seq
    low_width = rank // seq

    low_rank = sum_over(jnp.dot(tokens, low_in, preferred_element_type=F32), "feat").astype(BF16)
    partners = [swap(tokens, "feat", 1 << r) for r in range(remote)]

    def halves(wide, parts):
        return wide.T.reshape(parts, pairs, 2, -1, rows)

    def side_of(array, which):
        return lax.dynamic_index_in_dim(array, which, 2, keepdims=False)

    own_t = halves(tokens, per_dev)
    far_own = swap(side_of(own_t, 1 - side), "seq", 1)
    far = [far_own] + [swap(far_own, "feat", 1 << r) for r in range(remote)]
    near = [side_of(own_t, side)] + [side_of(halves(p, per_dev), side) for p in partners]
    both = [jnp.concatenate([n, f], axis=-1) for n, f in zip(near, far)]
    rank_t = halves(low_rank, 1)
    both_rank = jnp.concatenate(
        [side_of(rank_t, side), swap(side_of(rank_t, 1 - side), "seq", 1)], axis=-1
    )[0]

    activated, grad_pre = forward(tokens, partners, low_rank, butterfly, low_out, cotangent)

    weight_rows = []
    for k in range(per_dev):
        grads = jnp.concatenate([grad_pre[k], swap(grad_pre[k], "seq", 1)], axis=0)
        picks = [both[0][k]] + [both[0][k ^ 1 << b] for b in range(local_bits)]
        picks += [both[1 + r][k] for r in range(remote)]
        left = jnp.concatenate(picks + [both_rank], axis=1)
        deep = left.shape[1]
        terms = jnp.dot(
            left.reshape(pairs * deep, 2 * rows), grads, preferred_element_type=F32
        ).astype(BF16)
        weight_rows.append(line_scatter(terms.reshape(pairs, deep, hidden), place, pairs))
    butterfly_grad = jnp.stack(
        [w[: slots * width].reshape(slots, width, hidden) for w in weight_rows], axis=0
    )
    low_out_grad = jnp.concatenate([w[slots * width :] for w in weight_rows], axis=1)

    low_back = sum(
        dot_t(grad_pre[k], low_out[:, k * hidden : (k + 1) * hidden]) for k in range(per_dev)
    )
    low_grad = sum_over(low_back, "feat").astype(BF16)
    in_terms = lax.dot_general(
        low_grad, tokens, (((0,), (0,)), ((), ())), preferred_element_type=F32
    ).reshape(pairs, 2, low_width, per_dev * block)
    in_own = lax.dynamic_index_in_dim(in_terms, side, 1, keepdims=False)
    in_far = lax.dynamic_index_in_dim(in_terms, 1 - side, 1, keepdims=False).astype(BF16)
    in_pair = (in_own + swap(in_far, "seq", 1).astype(F32)).astype(BF16)
    low_in_grad = line_scatter(in_pair, place, pairs).T

    came = []
    for r in range(remote):
        slot = 1 + local_bits + r
        partial = [dot_t(grad_pre[k], butterfly[k, slot]).astype(BF16) for k in range(per_dev)]
        came.append(swap(jnp.concatenate(partial, axis=1), "feat", 1 << r))
    pieces = []
    for j in range(per_dev):
        at = slice(j * block, (j + 1) * block)
        total = dot_t(low_grad, low_in[at]) + dot_t(grad_pre[j], butterfly[j, 0])
        for b in range(local_bits):
            i = j ^ 1 << b
            total = total + dot_t(grad_pre[i], butterfly[i, 1 + b])
        for c in came:
            total = total + c[:, at].astype(F32)
        pieces.append(total.astype(BF16))
    tokens_grad = jnp.concatenate(pieces, axis=1)
    return (activated, tokens_grad, butterfly_grad, low_in_grad, low_out_grad)


def solution(mesh):
    placed = (
        P("seq", "feat"),
        P("feat", None, None, None),
        P("feat", None),
        P(None, "feat"),
        P("seq", "feat"),
    )
    return jax.shard_map(
        local,
        mesh=mesh,
        in_specs=placed,
        out_specs=(
            P("seq", "feat"),
            P("seq", "feat"),
            P("feat", None, "seq", None),
            P("feat", "seq"),
            P("seq", "feat"),
        ),
        check_vma=False,
    )
```

time: 950 us -> 444 us (0.47)
  waiting for transfers between devices: 677 us -> 214 us
  starting transfers between devices: 1.46 us -> 75.4 us
  local copies, waits for them, and re-layouts: 98.8 us -> 29.2 us
  blocking collectives: 43.7 us -> 0 us
  matrix products: 96 us -> 67.1 us
  Pallas kernels: 0 us -> 21.8 us
  other arithmetic: 15.3 us -> 33 us
  between operations: 13.9 us -> 1.95 us
    reduce_scatter x3 -> x0, waiting for transfers between devices: 567 us -> none  [the longest x1 567 us: local(): lax.psum_scatter(weight_terms, 'seq', scatter_dimension=2, tiled=True)]
    ppermute x2 -> x47, waiting for transfers between devices: 79.3 us -> 214 us  [the longest x30 121 us: line_scatter(): moving = lax.ppermute(term, 'seq', route)]
    ppermute x2 -> x47, starting transfers between devices: 1.3 us -> 75.4 us  [the longest x30 60.7 us: line_scatter(): moving = lax.ppermute(term, 'seq', route)]
    psum x2 -> x0, blocking collectives: 43.7 us -> none  [the longest x1 26.8 us: local(): low_rank = lax.psum(low_part, 'feat').astype(jnp.bfloat16)]
    reshape x4 -> x0, local copies, waits for them, and re-layouts: 33.5 us -> none  [the longest x1 12.3 us: local(): gathered = gathered.reshape(count_rows, total_blocks, block_width)]
    gather x6 -> x0, local copies, waits for them, and re-layouts: 31.6 us -> none  [the longest x4 21.5 us: local(): partners.append(jnp.take(gathered, picks, axis=1))]
    all_gather x1 -> x0, waiting for transfers between devices: 30.3 us -> none  [local(): gathered = lax.all_gather(tokens, 'feat', axis=1, tiled=True)]
    dot_general x10 -> x34, matrix products: 96 us -> 67.1 us  [the longest x28 45.5 us: dot_t(): lax.dot_general(left, right, (((1,), (1,)), ((), ())), preferred_element_...]
  transfers between devices with their start and end apart: 6 -> 47, of which waited for: 3 -> 18; matrix products, arithmetic and copies ran while one was open for 11% -> 27% of each run, Pallas kernels for 0% -> 5%
where the time goes in v1:
time: 444 us; the launch traced here: 442 us
  waiting for transfers between devices  214 us (48%)
  starting transfers between devices  75.4 us (17%)
  matrix products  67.1 us (15%)
  other arithmetic  33 us (7%)
  local copies, waits for them, and re-layouts  29.2 us (7%)
  Pallas kernels  21.8 us (5%)
    ppermute x30, waiting for transfers between devices, line_scatter(): moving = lax.ppermute(term, 'seq', route)  121 us
    ppermute x17, waiting for transfers between devices, swap(): return lax.ppermute(block, axis, [(i, i ^ distance) for i in range(count)])  92.3 us
    ppermute x30, starting transfers between devices, line_scatter(): moving = lax.ppermute(term, 'seq', route)  60.7 us
    dot_general x28, matrix products, dot_t(): lax.dot_general(left, right, (((1,), (1,)), ((), ())), preferred_element_...  45.5 us
    pallas_call x1, Pallas kernels, forward(): pl.pallas_call(functools.partial(forward_body, slots, tile), grid=(per_de...  21.8 us
    dot_general x4, matrix products, local(): jnp.dot(left.reshape(pairs * deep, 2 * rows), grads, preferred_element_ty...  17.4 us
    ppermute x17, starting transfers between devices, swap(): return lax.ppermute(block, axis, [(i, i ^ distance) for i in range(count)])  14.7 us
    unnamed x7, other arithmetic  10.3 us
  transfers between devices with their start and end apart: 47, of which 18 were waited for; matrix products, arithmetic and copies ran while one was open for 27% of the time, Pallas kernels for 5%

profile of v1, /device:TPU:16, one launch (start us, length us, event | category | flops | bytes accessed | tf_op | source)
XLA Modules:
  0.0 442.0 jit_solution(7677076761570062383)
XLA Ops:
  0.6 3.5 fusion.147
  6.2 2.5 copy.17
  8.7 2.7 dynamic-slice_bitcast_fusion.3
  12.9 2.1 add.274
  15.4 48.1 %collective-permute-done.3 = f32[512,256]{1,0:T(8,128)} collective-permute-done((f32[512,256]{1,0:T(8,128)}, f32[512,256]{1,0:T(8,128)}, u32[]{:S(2)}, u32[]{:S(2)}) %collective-permute-start.3) | collective-permute-done | bytes 524320 | tf_op jit(solution)/shard_map/ppermute | solution.py:16
  79.5 21.8 %shard_map.92 = (bf16[512,3584]{1,0:T(8,128)(2,1)}, bf16[4,512,896]{2,1,0:T(8,128)(2,1)}) custom-call(bf16[512,2048]{1,0:T(8,128)(2,1)S(1)} %copy-done, bf16[512,2048]{1,0:T(8,128)(2,1)S(1)} %copy-done, bf16[512,2048]{1,0:T(8,128)(2,1)S(1)} %copy-done, bf16[512,2048]{1,0:T(8,128)(2,1)} %collective-permute-done.refs_3_, ...), custom_call_target="tpu_custom_call" | custom-call | flops 10334765056 | bytes 39845888 | tf_op jit(solution)/shard_map/pallas_call | solution.py:77
  101.2 3.8 slice_bitcast_fusion.3
  105.5 2.9 fusion.73
  110.4 1.9 convolution_convert_fusion.11
  112.3 1.9 convolution_convert_fusion.8
  114.2 1.9 convolution_convert_fusion.9
  116.2 1.9 convolution_convert_fusion.4
  118.1 1.9 convolution_convert_fusion.5
  120.0 1.9 convolution_convert_fusion.6
  121.9 1.9 convolution_convert_fusion.7
  128.3 3.9 copy.18
  132.2 3.9 copy.19
  139.0 2.2 fusion.75
  141.2 2.1 fusion.60
  143.3 2.1 fusion.62
  146.2 2.4 fusion.112
  150.1 2.1 fusion.55
  152.2 2.1 fusion.57
  154.4 2.1 fusion.50
  160.4 1.9 fusion.52
  163.3 4.9 %convolution_convert_fusion.3 = bf16[1408,896]{1,0:T(8,128)(2,1)S(1)} fusion(bf16[1408,1024]{1,0:T(8,128)(2,1)S(1)} %bitcast.347, bf16[512,896]{1,0:T(8,128)(2,1)} %collective-permute-done.12, bf16[512,896]{1,0:T(8,128)(2,1)} %get-tuple-element.21), kind=kOutput, calls=%fused_computation.4 | convolution fusion | flops 2588622848 | bytes 7241728 | tf_op jit(solution)/shard_map/dot_general | solution.py:148
  169.8 4.5 %convolution_convert_fusion.2 = bf16[1408,896]{1,0:T(8,128)(2,1)S(1)} fusion(bf16[1408,1024]{1,0:T(8,128)(2,1)S(1)} %bitcast.348, bf16[512,896]{1,0:T(8,128)(2,1)} %copy-done.30, bf16[512,896]{1,0:T(8,128)(2,1)S(1)} %copy-done.20), kind=kOutput, calls=%fused_computation.3 | convolution fusion | flops 2588622848 | bytes 7241728 | tf_op jit(solution)/shard_map/dot_general | solution.py:148
  176.3 10.4 %collective-permute-done.26 = bf16[512,896]{1,0:T(8,128)(2,1)} collective-permute-done((bf16[512,896]{1,0:T(8,128)(2,1)S(1)}, bf16[512,896]{1,0:T(8,128)(2,1)}, u32[]{:S(2)}, u32[]{:S(2)}) %collective-permute-start.26) | collective-permute-done | bytes 917536 | tf_op jit(solution)/shard_map/ppermute | solution.py:16
  187.5 4.6 %convolution_convert_fusion.1 = bf16[1408,896]{1,0:T(8,128)(2,1)S(1)} fusion(bf16[1408,1024]{1,0:T(8,128)(2,1)S(1)} %bitcast.345, bf16[512,896]{1,0:T(8,128)(2,1)} %collective-permute-done.26, bf16[512,896]{1,0:T(8,128)(2,1)S(1)} %copy-done.19), kind=kOutput, calls=%fused_computation.2 | convolution fusion | flops 2588622848 | bytes 7241728 | tf_op jit(solution)/shard_map/dot_general | solution.py:148
  193.1 12.5 %collective-permute-done.33 = bf16[512,896]{1,0:T(8,128)(2,1)S(1)} collective-permute-done((bf16[512,896]{1,0:T(8,128)(2,1)S(1)}, bf16[512,896]{1,0:T(8,128)(2,1)S(1)}, u32[]{:S(2)}, u32[]{:S(2)}) %collective-permute-start.33) | collective-permute-done | bytes 917536 | tf_op jit(solution)/shard_map/ppermute | solution.py:16
  206.3 3.4 convolution_convert_fusion
  209.8 12.0 %collective-permute-done.5 = f32[512,256]{1,0:T(8,128)S(1)} collective-permute-done((f32[512,256]{1,0:T(8,128)S(1)}, f32[512,256]{1,0:T(8,128)S(1)}, u32[]{:S(2)}, u32[]{:S(2)}) %collective-permute-start.5) | collective-permute-done | bytes 524320 | tf_op jit(solution)/shard_map/ppermute | solution.py:16
  227.0 9.2 %collective-permute-done.40 = bf16[4,32,2048]{2,1,0:T(8,128)(2,1)S(1)} collective-permute-done((bf16[4,32,2048]{2,1,0:T(8,128)(2,1)S(1)}, bf16[4,32,2048]{2,1,0:T(8,128)(2,1)S(1)}, u32[]{:S(2)}, u32[]{:S(2)}) %collective-permute-start.40) | collective-permute-done | bytes 524320 | tf_op jit(solution)/shard_map/ppermute | solution.py:16
  242.4 3.2 collective-permute-done.44
  246.9 17.8 %collective-permute-done.42 = bf16[32,2048]{1,0:T(8,128)(2,1)S(1)} collective-permute-done((bf16[32,2048]{1,0:T(8,128)(2,1)S(1)}, bf16[32,2048]{1,0:T(8,128)(2,1)S(1)}, u32[]{:S(2)}, u32[]{:S(2)}) %collective-permute-start.42) | collective-permute-done | bytes 131104 | tf_op jit(solution)/shard_map/ppermute | solution.py:40
  266.1 4.1 collective-permute-start.45
  271.3 12.0 %collective-permute-done.45 = bf16[32,2048]{1,0:T(8,128)(2,1)S(1)} collective-permute-done((bf16[32,2048]{1,0:T(8,128)(2,1)S(1)}, bf16[32,2048]{1,0:T(8,128)(2,1)S(1)}, u32[]{:S(2)}, u32[]{:S(2)}) %collective-permute-start.45) | collective-permute-done | bytes 131104 | tf_op jit(solution)/shard_map/ppermute | solution.py:40
  284.6 1.9 collective-permute-start.43
  286.6 4.6 %collective-permute-start.46 = (bf16[32,2048]{1,0:T(8,128)(2,1)S(1)}, bf16[32,2048]{1,0:T(8,128)(2,1)}, u32[]{:S(2)}, u32[]{:S(2)}) collective-permute-start(bf16[32,2048]{1,0:T(8,128)(2,1)S(1)} %fusion.133), channel_id=1, source_target_pairs={{8,0},{12,4},{16,8},{20,12},{24,16},{28,20},{9,1},{13,5},{17,9},{2... | collective-permute-start | bytes 393224 | tf_op jit(solution)/shard_map/ppermute | solution.py:40
  291.1 2.1 fusion.24
  293.3 2.1 fusion.25
  295.4 2.1 fusion.26
  297.5 2.1 fusion.27
  299.8 2.4 copy.22
  310.7 2.0 fusion.46
  312.7 10.2 %collective-permute-done.21 = bf16[352,896]{1,0:T(8,128)(2,1)S(1)} collective-permute-done((bf16[352,896]{1,0:T(8,128)(2,1)}, bf16[352,896]{1,0:T(8,128)(2,1)S(1)}, u32[]{:S(2)}, u32[]{:S(2)}) %collective-permute-start.21) | collective-permute-done | bytes 630816 | tf_op jit(solution)/shard_map/ppermute | solution.py:40
  322.9 4.0 collective-permute-start.17
  328.4 2.0 collective-permute-start.15
  330.4 6.0 %collective-permute-done.28 = bf16[352,896]{1,0:T(8,128)(2,1)S(1)} collective-permute-done((bf16[352,896]{1,0:T(8,128)(2,1)}, bf16[352,896]{1,0:T(8,128)(2,1)S(1)}, u32[]{:S(2)}, u32[]{:S(2)}) %collective-permute-start.28) | collective-permute-done | bytes 630816 | tf_op jit(solution)/shard_map/ppermute | solution.py:40
  336.4 4.0 collective-permute-start.24
  340.8 2.0 collective-permute-start.22
  342.8 7.2 %collective-permute-done.35 = bf16[352,896]{1,0:T(8,128)(2,1)S(1)} collective-permute-done((bf16[352,896]{1,0:T(8,128)(2,1)}, bf16[352,896]{1,0:T(8,128)(2,1)S(1)}, u32[]{:S(2)}, u32[]{:S(2)}) %collective-permute-start.35) | collective-permute-done | bytes 630816 | tf_op jit(solution)/shard_map/ppermute | solution.py:40
  349.9 3.9 collective-permute-start.31
  354.2 1.9 collective-permute-start.38
  356.3 5.8 %collective-permute-done.24 = bf16[352,896]{1,0:T(8,128)(2,1)S(1)} collective-permute-done((bf16[352,896]{1,0:T(8,128)(2,1)S(1)}, bf16[352,896]{1,0:T(8,128)(2,1)S(1)}, u32[]{:S(2)}, u32[]{:S(2)}) %collective-permute-start.24) | collective-permute-done | bytes 630816 | tf_op jit(solution)/shard_map/ppermute | solution.py:40
  364.2 11.4 %collective-permute-done.31 = bf16[352,896]{1,0:T(8,128)(2,1)S(1)} collective-permute-done((bf16[352,896]{1,0:T(8,128)(2,1)S(1)}, bf16[352,896]{1,0:T(8,128)(2,1)S(1)}, u32[]{:S(2)}, u32[]{:S(2)}) %collective-permute-start.31) | collective-permute-done | bytes 630816 | tf_op jit(solution)/shard_map/ppermute | solution.py:40
  377.7 4.0 collective-permute-start.29
  381.7 7.4 %collective-permute-done.38 = bf16[352,896]{1,0:T(8,128)(2,1)S(1)} collective-permute-done((bf16[352,896]{1,0:T(8,128)(2,1)S(1)}, bf16[352,896]{1,0:T(8,128)(2,1)S(1)}, u32[]{:S(2)}, u32[]{:S(2)}) %collective-permute-start.38) | collective-permute-done | bytes 630816 | tf_op jit(solution)/shard_map/ppermute | solution.py:40
  391.3 3.9 collective-permute-start.36
  395.2 7.4 %collective-permute-done.18 = bf16[352,896]{1,0:T(8,128)(2,1)S(1)} collective-permute-done((bf16[352,896]{1,0:T(8,128)(2,1)S(1)}, bf16[352,896]{1,0:T(8,128)(2,1)S(1)}, u32[]{:S(2)}, u32[]{:S(2)}) %collective-permute-start.18) | collective-permute-done | bytes 630816 | tf_op jit(solution)/shard_map/ppermute | solution.py:40
  404.8 11.4 %collective-permute-done.25 = bf16[352,896]{1,0:T(8,128)(2,1)S(1)} collective-permute-done((bf16[352,896]{1,0:T(8,128)(2,1)S(1)}, bf16[352,896]{1,0:T(8,128)(2,1)S(1)}, u32[]{:S(2)}, u32[]{:S(2)}) %collective-permute-start.25) | collective-permute-done | bytes 630816 | tf_op jit(solution)/shard_map/ppermute | solution.py:40
  416.5 13.2 %collective-permute-done.32 = bf16[352,896]{1,0:T(8,128)(2,1)S(1)} collective-permute-done((bf16[352,896]{1,0:T(8,128)(2,1)S(1)}, bf16[352,896]{1,0:T(8,128)(2,1)S(1)}, u32[]{:S(2)}, u32[]{:S(2)}) %collective-permute-start.32) | collective-permute-done | bytes 630816 | tf_op jit(solution)/shard_map/ppermute | solution.py:40
  430.1 8.2 %collective-permute-done.39 = bf16[352,896]{1,0:T(8,128)(2,1)S(1)} collective-permute-done((bf16[352,896]{1,0:T(8,128)(2,1)S(1)}, bf16[352,896]{1,0:T(8,128)(2,1)S(1)}, u32[]{:S(2)}, u32[]{:S(2)}) %collective-permute-start.39) | collective-permute-done | bytes 630816 | tf_op jit(solution)/shard_map/ppermute | solution.py:40
  439.5 2.5 pad_maximum_fusion
  (195 shorter events, 80.1 us)
Async XLA Ops:
  4.2 8.7 %collective-permute-start.2 = (f32[512,256]{1,0:T(8,128)}, f32[512,256]{1,0:T(8,128)}, u32[]{:S(2)}, u32[]{:S(2)}) collective-permute-start(f32[512,256]{1,0:T(8,128)} %fusion.147), channel_id=1, source_target_pairs={{0,1},{1,0},{2,3},{3,2},{4,5},{5,4},{6,7},{7,6},{8,9},{9,8},{10,11... | collective-permute-start | bytes 1572872 | tf_op jit(solution)/shard_map/ppermute | solution.py:16
  4.2 74.4 %collective-permute-start = (bf16[512,2048]{1,0:T(8,128)(2,1)S(1)}, bf16[512,2048]{1,0:T(8,128)(2,1)}, u32[]{:S(2)}, u32[]{:S(2)}) collective-permute-start(bf16[512,2048]{1,0:T(8,128)(2,1)S(1)} %copy-done), channel_id=1, source_target_pairs={{0,1},{1,0},{2,3},{3,2},{4,5},{5,4},{6,7},{7,6},{8,9},{9,8},{10,11... | collective-permute-start | bytes 6291464 | tf_op jit(solution)/shard_map/ppermute | solution.py:16
  4.7 73.9 %collective-permute-start.1 = (bf16[512,2048]{1,0:T(8,128)(2,1)S(1)}, bf16[512,2048]{1,0:T(8,128)(2,1)}, u32[]{:S(2)}, u32[]{:S(2)}) collective-permute-start(bf16[512,2048]{1,0:T(8,128)(2,1)S(1)} %copy-done), channel_id=1, source_target_pairs={{0,2},{1,3},{2,0},{3,1},{4,6},{5,7},{6,4},{7,5},{8,10},{9,11},{10,... | collective-permute-start | bytes 6291464 | tf_op jit(solution)/shard_map/ppermute | solution.py:16
  11.4 57.4 %collective-permute-start.8 = (bf16[4,4,64,512]{3,2,1,0:T(8,128)(2,1)}, bf16[4,4,64,512]{3,2,1,0:T(8,128)(2,1)}, u32[]{:S(2)}, u32[]{:S(2)}) collective-permute-start(bf16[4,4,64,512]{3,2,1,0:T(8,128)(2,1)} %get-tuple-element.59), channel_id=1, source_target_pairs={{0,4},{4,0},{8,12},{12,8},{16,20},{20,16},{24,28},{28,24},{1,5},{5... | collective-permute-start | bytes 3145736 | tf_op jit(solution)/shard_map/ppermute | solution.py:16
  14.9 48.6 %collective-permute-start.3 = (f32[512,256]{1,0:T(8,128)}, f32[512,256]{1,0:T(8,128)}, u32[]{:S(2)}, u32[]{:S(2)}) collective-permute-start(f32[512,256]{1,0:T(8,128)} %add.274), channel_id=1, source_target_pairs={{0,2},{1,3},{2,0},{3,1},{4,6},{5,7},{6,4},{7,5},{8,10},{9,11},{10,... | collective-permute-start | bytes 1572872 | tf_op jit(solution)/shard_map/ppermute | solution.py:16
  67.3 90.7 %collective-permute-start.11 = (bf16[1,4,32,512]{3,2,1,0:T(8,128)(2,1)}, bf16[1,4,32,512]{3,2,1,0:T(8,128)(2,1)}, u32[]{:S(2)}, u32[]{:S(2)}) collective-permute-start(bf16[1,4,32,512]{3,2,1,0:T(8,128)(2,1)} %get-tuple-element.69), channel_id=1, source_target_pairs={{0,4},{4,0},{8,12},{12,8},{16,20},{20,16},{24,28},{28,24},{1,5},{5... | collective-permute-start | bytes 393224 | tf_op jit(solution)/shard_map/ppermute | solution.py:16
  68.8 76.5 %collective-permute-start.9 = (bf16[4,4,64,512]{3,2,1,0:T(8,128)(2,1)}, bf16[4,4,64,512]{3,2,1,0:T(8,128)(2,1)}, u32[]{:S(2)}, u32[]{:S(2)}) collective-permute-start(bf16[4,4,64,512]{3,2,1,0:T(8,128)(2,1)} %collective-permute-done.8), channel_id=1, source_target_pairs={{0,1},{1,0},{2,3},{3,2},{4,5},{5,4},{6,7},{7,6},{8,9},{9,8},{10,11... | collective-permute-start | bytes 3145736 | tf_op jit(solution)/shard_map/ppermute | solution.py:16
  68.8 87.7 %collective-permute-start.10 = (bf16[4,4,64,512]{3,2,1,0:T(8,128)(2,1)}, bf16[4,4,64,512]{3,2,1,0:T(8,128)(2,1)}, u32[]{:S(2)}, u32[]{:S(2)}) collective-permute-start(bf16[4,4,64,512]{3,2,1,0:T(8,128)(2,1)} %collective-permute-done.8), channel_id=1, source_target_pairs={{0,2},{1,3},{2,0},{3,1},{4,6},{5,7},{6,4},{7,5},{8,10},{9,11},{10,... | collective-permute-start | bytes 3145736 | tf_op jit(solution)/shard_map/ppermute | solution.py:16
  76.7 24.5 %copy-start.26 = (bf16[4,352,1024]{2,1,0:T(8,128)(2,1)}, bf16[4,352,1024]{2,1,0:T(8,128)(2,1)S(1)}, u32[]{:S(2)}) copy-start(bf16[4,352,1024]{2,1,0:T(8,128)(2,1)S(1)} %get-tuple-element.49) | copy-start | bytes 8650756
  78.6 22.7 %copy-start.22 = (bf16[4,352,1024]{2,1,0:T(8,128)(2,1)}, bf16[4,352,1024]{2,1,0:T(8,128)(2,1)S(1)}, u32[]{:S(2)}) copy-start(bf16[4,352,1024]{2,1,0:T(8,128)(2,1)S(1)} %get-tuple-element.56) | copy-start | bytes 8650756
  78.6 22.6 %copy-start.24 = (bf16[4,352,1024]{2,1,0:T(8,128)(2,1)}, bf16[4,352,1024]{2,1,0:T(8,128)(2,1)S(1)}, u32[]{:S(2)}) copy-start(bf16[4,352,1024]{2,1,0:T(8,128)(2,1)S(1)} %get-tuple-element.57) | copy-start | bytes 8650756
  123.9 38.8 %collective-permute-start.12 = (bf16[512,896]{1,0:T(8,128)(2,1)}, bf16[512,896]{1,0:T(8,128)(2,1)}, u32[]{:S(2)}, u32[]{:S(2)}) collective-permute-start(bf16[512,896]{1,0:T(8,128)(2,1)} %get-tuple-element.21), channel_id=1, source_target_pairs={{0,4},{4,0},{8,12},{12,8},{16,20},{20,16},{24,28},{28,24},{1,5},{5... | collective-permute-start | bytes 2752520 | tf_op jit(solution)/shard_map/ppermute | solution.py:16
  136.2 32.0 %collective-permute-start.19 = (bf16[512,896]{1,0:T(8,128)(2,1)}, bf16[512,896]{1,0:T(8,128)(2,1)S(1)}, u32[]{:S(2)}, u32[]{:S(2)}) collective-permute-start(bf16[512,896]{1,0:T(8,128)(2,1)} %get-tuple-element.24), channel_id=1, source_target_pairs={{0,4},{4,0},{8,12},{12,8},{16,20},{20,16},{24,28},{28,24},{1,5},{5... | collective-permute-start | bytes 2752520 | tf_op jit(solution)/shard_map/ppermute | solution.py:16
  145.4 41.4 %collective-permute-start.26 = (bf16[512,896]{1,0:T(8,128)(2,1)S(1)}, bf16[512,896]{1,0:T(8,128)(2,1)}, u32[]{:S(2)}, u32[]{:S(2)}) collective-permute-start(bf16[512,896]{1,0:T(8,128)(2,1)S(1)} %copy-done.19), channel_id=1, source_target_pairs={{0,4},{4,0},{8,12},{12,8},{16,20},{20,16},{24,28},{28,24},{1,5},{5... | collective-permute-start | bytes 2752520 | tf_op jit(solution)/shard_map/ppermute | solution.py:16
  156.5 5.8 %collective-permute-start.4 = (f32[512,256]{1,0:T(8,128)S(1)}, f32[512,256]{1,0:T(8,128)S(1)}, u32[]{:S(2)}, u32[]{:S(2)}) collective-permute-start(f32[512,256]{1,0:T(8,128)S(1)} %convolution_add_fusion.8), channel_id=1, source_target_pairs={{0,1},{1,0},{2,3},{3,2},{4,5},{5,4},{6,7},{7,6},{8,9},{9,8},{10,11... | collective-permute-start | bytes 1572872 | tf_op jit(solution)/shard_map/ppermute | solution.py:16
  158.0 47.6 %collective-permute-start.33 = (bf16[512,896]{1,0:T(8,128)(2,1)S(1)}, bf16[512,896]{1,0:T(8,128)(2,1)S(1)}, u32[]{:S(2)}, u32[]{:S(2)}) collective-permute-start(bf16[512,896]{1,0:T(8,128)(2,1)S(1)} %get-tuple-element.22), channel_id=1, source_target_pairs={{0,4},{4,0},{8,12},{12,8},{16,20},{20,16},{24,28},{28,24},{1,5},{5... | collective-permute-start | bytes 2752520 | tf_op jit(solution)/shard_map/ppermute | solution.py:16
  162.3 122.3 %collective-permute-start.6 = (bf16[512,2048]{0,1:T(8,128)(2,1)S(1)}, bf16[512,2048]{0,1:T(8,128)(2,1)S(1)}, u32[]{:S(2)}, u32[]{:S(2)}) collective-permute-start(bf16[512,2048]{0,1:T(8,128)(2,1)S(1)} %copy-done.16), channel_id=1, source_target_pairs={{0,1},{1,0},{2,3},{3,2},{4,5},{5,4},{6,7},{7,6},{8,9},{9,8},{10,11... | collective-permute-start | bytes 6291464 | tf_op jit(solution)/shard_map/ppermute | solution.py:16
  162.7 123.9 %collective-permute-start.7 = (bf16[512,2048]{0,1:T(8,128)(2,1)S(1)}, bf16[512,2048]{0,1:T(8,128)(2,1)}, u32[]{:S(2)}, u32[]{:S(2)}) collective-permute-start(bf16[512,2048]{0,1:T(8,128)(2,1)S(1)} %copy-done.15), channel_id=1, source_target_pairs={{0,2},{1,3},{2,0},{3,1},{4,6},{5,7},{6,4},{7,5},{8,10},{9,11},{10,... | collective-permute-start | bytes 6291464 | tf_op jit(solution)/shard_map/ppermute | solution.py:16
  168.2 57.8 %copy-start.4 = (bf16[1408,896]{1,0:T(8,128)(2,1)}, bf16[1408,896]{1,0:T(8,128)(2,1)S(1)}, u32[]{:S(2)}) copy-start(bf16[1408,896]{1,0:T(8,128)(2,1)S(1)} %convolution_convert_fusion.3) | copy-start | bytes 7569412
  168.2 53.6 %collective-permute-start.5 = (f32[512,256]{1,0:T(8,128)S(1)}, f32[512,256]{1,0:T(8,128)S(1)}, u32[]{:S(2)}, u32[]{:S(2)}) collective-permute-start(f32[512,256]{1,0:T(8,128)S(1)} %add.279), channel_id=1, source_target_pairs={{0,2},{1,3},{2,0},{3,1},{4,6},{5,7},{6,4},{7,5},{8,10},{9,11},{10,... | collective-permute-start | bytes 1572872 | tf_op jit(solution)/shard_map/ppermute | solution.py:16
  174.3 63.4 %copy-start.6 = (bf16[1408,896]{1,0:T(8,128)(2,1)}, bf16[1408,896]{1,0:T(8,128)(2,1)S(1)}, u32[]{:S(2)}) copy-start(bf16[1408,896]{1,0:T(8,128)(2,1)S(1)} %convolution_convert_fusion.2) | copy-start | bytes 7569412
  186.8 38.3 %collective-permute-start.13 = (bf16[352,896]{1,0:T(8,128)(2,1)S(1)}, bf16[352,896]{1,0:T(8,128)(2,1)S(1)}, u32[]{:S(2)}, u32[]{:S(2)}) collective-permute-start(bf16[352,896]{1,0:T(8,128)(2,1)S(1)} %get-tuple-element.27), channel_id=1, source_target_pairs={{0,8},{4,12},{1,9},{5,13},{2,10},{6,14},{3,11},{7,15}} | collective-permute-start | bytes 1892360 | tf_op jit(solution)/shard_map/ppermute | solution.py:40
  192.0 49.4 %copy-start.10 = (bf16[1408,896]{1,0:T(8,128)(2,1)}, bf16[1408,896]{1,0:T(8,128)(2,1)S(1)}, u32[]{:S(2)}) copy-start(bf16[1408,896]{1,0:T(8,128)(2,1)S(1)} %convolution_convert_fusion.1) | copy-start | bytes 7569412
  205.6 31.4 %collective-permute-start.20 = (bf16[352,896]{1,0:T(8,128)(2,1)S(1)}, bf16[352,896]{1,0:T(8,128)(2,1)S(1)}, u32[]{:S(2)}, u32[]{:S(2)}) collective-permute-start(bf16[352,896]{1,0:T(8,128)(2,1)S(1)} %get-tuple-element.31), channel_id=1, source_target_pairs={{0,8},{4,12},{1,9},{5,13},{2,10},{6,14},{3,11},{7,15}} | collective-permute-start | bytes 1892360 | tf_op jit(solution)/shard_map/ppermute | solution.py:40
  209.7 60.6 %copy-start.8 = (bf16[1408,896]{1,0:T(8,128)(2,1)}, bf16[1408,896]{1,0:T(8,128)(2,1)S(1)}, u32[]{:S(2)}) copy-start(bf16[1408,896]{1,0:T(8,128)(2,1)S(1)} %convolution_convert_fusion) | copy-start | bytes 7569412
  222.8 13.4 %collective-permute-start.40 = (bf16[4,32,2048]{2,1,0:T(8,128)(2,1)S(1)}, bf16[4,32,2048]{2,1,0:T(8,128)(2,1)S(1)}, u32[]{:S(2)}, u32[]{:S(2)}) collective-permute-start(bf16[4,32,2048]{2,1,0:T(8,128)(2,1)S(1)} %fusion.97), channel_id=1, source_target_pairs={{0,4},{4,0},{8,12},{12,8},{16,20},{20,16},{24,28},{28,24},{1,5},{5... | collective-permute-start | bytes 1572872 | tf_op jit(solution)/shard_map/ppermute | solution.py:16
  225.1 15.0 %collective-permute-start.27 = (bf16[352,896]{1,0:T(8,128)(2,1)S(1)}, bf16[352,896]{1,0:T(8,128)(2,1)S(1)}, u32[]{:S(2)}, u32[]{:S(2)}) collective-permute-start(bf16[352,896]{1,0:T(8,128)(2,1)S(1)} %get-tuple-element.35), channel_id=1, source_target_pairs={{0,8},{4,12},{1,9},{5,13},{2,10},{6,14},{3,11},{7,15}} | collective-permute-start | bytes 1892360 | tf_op jit(solution)/shard_map/ppermute | solution.py:40
  236.2 29.9 %collective-permute-start.34 = (bf16[352,896]{1,0:T(8,128)(2,1)S(1)}, bf16[352,896]{1,0:T(8,128)(2,1)S(1)}, u32[]{:S(2)}, u32[]{:S(2)}) collective-permute-start(bf16[352,896]{1,0:T(8,128)(2,1)S(1)} %get-tuple-element.39), channel_id=1, source_target_pairs={{0,8},{4,12},{1,9},{5,13},{2,10},{6,14},{3,11},{7,15}} | collective-permute-start | bytes 1892360 | tf_op jit(solution)/shard_map/ppermute | solution.py:40
  237.0 1.7 collective-permute-start.41
  238.7 6.9 %collective-permute-start.44 = (bf16[32,2048]{1,0:T(8,128)(2,1)S(1)}, bf16[32,2048]{1,0:T(8,128)(2,1)S(1)}, u32[]{:S(2)}, u32[]{:S(2)}) collective-permute-start(bf16[32,2048]{1,0:T(8,128)(2,1)S(1)} %get-tuple-element.63), channel_id=1, source_target_pairs={{24,16},{28,20},{25,17},{29,21},{26,18},{30,22},{27,19},{31,23}} | collective-permute-start | bytes 393224 | tf_op jit(solution)/shard_map/ppermute | solution.py:40
  240.1 24.6 %collective-permute-start.42 = (bf16[32,2048]{1,0:T(8,128)(2,1)S(1)}, bf16[32,2048]{1,0:T(8,128)(2,1)S(1)}, u32[]{:S(2)}, u32[]{:S(2)}) collective-permute-start(bf16[32,2048]{1,0:T(8,128)(2,1)S(1)} %fusion.134), channel_id=1, source_target_pairs={{0,8},{4,12},{8,16},{12,20},{1,9},{5,13},{9,17},{13,21},{2,10},{6,... | collective-permute-start | bytes 393224 | tf_op jit(solution)/shard_map/ppermute | solution.py:40
  245.6 56.6 %collective-permute-start.16 = (bf16[352,896]{1,0:T(8,128)(2,1)}, bf16[352,896]{1,0:T(8,128)(2,1)}, u32[]{:S(2)}, u32[]{:S(2)}) collective-permute-start(bf16[352,896]{1,0:T(8,128)(2,1)} %get-tuple-element.28), channel_id=1, source_target_pairs={{24,16},{28,20},{25,17},{29,21},{26,18},{30,22},{27,19},{31,23}} | collective-permute-start | bytes 1892360 | tf_op jit(solution)/shard_map/ppermute | solution.py:40
  264.7 43.2 %collective-permute-start.23 = (bf16[352,896]{1,0:T(8,128)(2,1)}, bf16[352,896]{1,0:T(8,128)(2,1)}, u32[]{:S(2)}, u32[]{:S(2)}) collective-permute-start(bf16[352,896]{1,0:T(8,128)(2,1)} %get-tuple-element.32), channel_id=1, source_target_pairs={{24,16},{28,20},{25,17},{29,21},{26,18},{30,22},{27,19},{31,23}} | collective-permute-start | bytes 1892360 | tf_op jit(solution)/shard_map/ppermute | solution.py:40
  266.1 17.2 %collective-permute-start.45 = (bf16[32,2048]{1,0:T(8,128)(2,1)S(1)}, bf16[32,2048]{1,0:T(8,128)(2,1)S(1)}, u32[]{:S(2)}, u32[]{:S(2)}) collective-permute-start(bf16[32,2048]{1,0:T(8,128)(2,1)S(1)} %get-tuple-element.61), channel_id=1, source_target_pairs={{16,8},{20,12},{24,16},{28,20},{17,9},{21,13},{25,17},{29,21},{18,... | collective-permute-start | bytes 393224 | tf_op jit(solution)/shard_map/ppermute | solution.py:40
  283.3 26.1 %collective-permute-start.14 = (bf16[352,896]{1,0:T(8,128)(2,1)}, bf16[352,896]{1,0:T(8,128)(2,1)}, u32[]{:S(2)}, u32[]{:S(2)}) collective-permute-start(bf16[352,896]{1,0:T(8,128)(2,1)} %fusion.45), channel_id=1, source_target_pairs={{0,8},{4,12},{8,16},{12,20},{1,9},{5,13},{9,17},{13,21},{2,10},{6,... | collective-permute-start | bytes 1892360 | tf_op jit(solution)/shard_map/ppermute | solution.py:40
  284.6 19.0 %collective-permute-start.43 = (bf16[32,2048]{1,0:T(8,128)(2,1)S(1)}, bf16[32,2048]{1,0:T(8,128)(2,1)}, u32[]{:S(2)}, u32[]{:S(2)}) collective-permute-start(bf16[32,2048]{1,0:T(8,128)(2,1)S(1)} %get-tuple-element.60), channel_id=1, source_target_pairs={{0,8},{4,12},{8,16},{12,20},{16,24},{20,28},{1,9},{5,13},{9,17},{1... | collective-permute-start | bytes 393224 | tf_op jit(solution)/shard_map/ppermute | solution.py:40
  286.6 18.4 %collective-permute-start.46 = (bf16[32,2048]{1,0:T(8,128)(2,1)S(1)}, bf16[32,2048]{1,0:T(8,128)(2,1)}, u32[]{:S(2)}, u32[]{:S(2)}) collective-permute-start(bf16[32,2048]{1,0:T(8,128)(2,1)S(1)} %fusion.133), channel_id=1, source_target_pairs={{8,0},{12,4},{16,8},{20,12},{24,16},{28,20},{9,1},{13,5},{17,9},{2... | collective-permute-start | bytes 393224 | tf_op jit(solution)/shard_map/ppermute | solution.py:40
  302.2 24.8 %copy-start.7 = (bf16[1408,896]{1,0:T(8,128)(2,1)S(1)}, bf16[1408,896]{1,0:T(8,128)(2,1)}, u32[]{:S(2)}) copy-start(bf16[1408,896]{1,0:T(8,128)(2,1)} %copy-done.6) | copy-start | bytes 7569412
  302.2 26.2 %collective-permute-start.30 = (bf16[352,896]{1,0:T(8,128)(2,1)}, bf16[352,896]{1,0:T(8,128)(2,1)S(1)}, u32[]{:S(2)}, u32[]{:S(2)}) collective-permute-start(bf16[352,896]{1,0:T(8,128)(2,1)} %get-tuple-element.36), channel_id=1, source_target_pairs={{24,16},{28,20},{25,17},{29,21},{26,18},{30,22},{27,19},{31,23}} | collective-permute-start | bytes 1892360 | tf_op jit(solution)/shard_map/ppermute | solution.py:40
  303.6 19.3 %collective-permute-start.21 = (bf16[352,896]{1,0:T(8,128)(2,1)}, bf16[352,896]{1,0:T(8,128)(2,1)S(1)}, u32[]{:S(2)}, u32[]{:S(2)}) collective-permute-start(bf16[352,896]{1,0:T(8,128)(2,1)} %fusion.40), channel_id=1, source_target_pairs={{0,8},{4,12},{8,16},{12,20},{1,9},{5,13},{9,17},{13,21},{2,10},{6,... | collective-permute-start | bytes 1892360 | tf_op jit(solution)/shard_map/ppermute | solution.py:40
  304.9 31.5 %collective-permute-start.28 = (bf16[352,896]{1,0:T(8,128)(2,1)}, bf16[352,896]{1,0:T(8,128)(2,1)S(1)}, u32[]{:S(2)}, u32[]{:S(2)}) collective-permute-start(bf16[352,896]{1,0:T(8,128)(2,1)} %fusion.35), channel_id=1, source_target_pairs={{0,8},{4,12},{8,16},{12,20},{1,9},{5,13},{9,17},{13,21},{2,10},{6,... | collective-permute-start | bytes 1892360 | tf_op jit(solution)/shard_map/ppermute | solution.py:40
  308.0 32.5 %copy-start.11 = (bf16[1408,896]{1,0:T(8,128)(2,1)S(1)}, bf16[1408,896]{1,0:T(8,128)(2,1)}, u32[]{:S(2)}) copy-start(bf16[1408,896]{1,0:T(8,128)(2,1)} %copy-done.10) | copy-start | bytes 7569412
  308.0 32.9 %collective-permute-start.37 = (bf16[352,896]{1,0:T(8,128)(2,1)S(1)}, bf16[352,896]{1,0:T(8,128)(2,1)S(1)}, u32[]{:S(2)}, u32[]{:S(2)}) collective-permute-start(bf16[352,896]{1,0:T(8,128)(2,1)S(1)} %get-tuple-element.40), channel_id=1, source_target_pairs={{24,16},{28,20},{25,17},{29,21},{26,18},{30,22},{27,19},{31,23}} | collective-permute-start | bytes 1892360 | tf_op jit(solution)/shard_map/ppermute | solution.py:40
  309.4 40.5 %collective-permute-start.35 = (bf16[352,896]{1,0:T(8,128)(2,1)}, bf16[352,896]{1,0:T(8,128)(2,1)S(1)}, u32[]{:S(2)}, u32[]{:S(2)}) collective-permute-start(bf16[352,896]{1,0:T(8,128)(2,1)} %fusion.30), channel_id=1, source_target_pairs={{0,8},{4,12},{8,16},{12,20},{1,9},{5,13},{9,17},{13,21},{2,10},{6,... | collective-permute-start | bytes 1892360 | tf_op jit(solution)/shard_map/ppermute | solution.py:40
  322.9 31.0 %copy-start.9 = (bf16[1408,896]{1,0:T(8,128)(2,1)S(1)}, bf16[1408,896]{1,0:T(8,128)(2,1)}, u32[]{:S(2)}) copy-start(bf16[1408,896]{1,0:T(8,128)(2,1)} %copy-done.8) | copy-start | bytes 7569412
  322.9 31.3 %collective-permute-start.17 = (bf16[352,896]{1,0:T(8,128)(2,1)S(1)}, bf16[352,896]{1,0:T(8,128)(2,1)S(1)}, u32[]{:S(2)}, u32[]{:S(2)}) collective-permute-start(bf16[352,896]{1,0:T(8,128)(2,1)S(1)} %get-tuple-element.26), channel_id=1, source_target_pairs={{16,8},{20,12},{24,16},{28,20},{17,9},{21,13},{25,17},{29,21},{18,... | collective-permute-start | bytes 1892360 | tf_op jit(solution)/shard_map/ppermute | solution.py:40
  328.4 49.3 %collective-permute-start.15 = (bf16[352,896]{1,0:T(8,128)(2,1)S(1)}, bf16[352,896]{1,0:T(8,128)(2,1)S(1)}, u32[]{:S(2)}, u32[]{:S(2)}) collective-permute-start(bf16[352,896]{1,0:T(8,128)(2,1)S(1)} %get-tuple-element.25), channel_id=1, source_target_pairs={{0,8},{4,12},{8,16},{12,20},{16,24},{20,28},{1,9},{5,13},{9,17},{1... | collective-permute-start | bytes 1892360 | tf_op jit(solution)/shard_map/ppermute | solution.py:40
  336.4 19.7 %copy-start.5 = (bf16[1408,896]{1,0:T(8,128)(2,1)S(1)}, bf16[1408,896]{1,0:T(8,128)(2,1)}, u32[]{:S(2)}) copy-start(bf16[1408,896]{1,0:T(8,128)(2,1)} %copy-done.4) | copy-start | bytes 7569412
  336.4 25.7 %collective-permute-start.24 = (bf16[352,896]{1,0:T(8,128)(2,1)S(1)}, bf16[352,896]{1,0:T(8,128)(2,1)S(1)}, u32[]{:S(2)}, u32[]{:S(2)}) collective-permute-start(bf16[352,896]{1,0:T(8,128)(2,1)S(1)} %get-tuple-element.30), channel_id=1, source_target_pairs={{16,8},{20,12},{24,16},{28,20},{17,9},{21,13},{25,17},{29,21},{18,... | collective-permute-start | bytes 1892360 | tf_op jit(solution)/shard_map/ppermute | solution.py:40
  340.8 50.4 %collective-permute-start.22 = (bf16[352,896]{1,0:T(8,128)(2,1)S(1)}, bf16[352,896]{1,0:T(8,128)(2,1)S(1)}, u32[]{:S(2)}, u32[]{:S(2)}) collective-permute-start(bf16[352,896]{1,0:T(8,128)(2,1)S(1)} %get-tuple-element.29), channel_id=1, source_target_pairs={{0,8},{4,12},{8,16},{12,20},{16,24},{20,28},{1,9},{5,13},{9,17},{1... | collective-permute-start | bytes 1892360 | tf_op jit(solution)/shard_map/ppermute | solution.py:40
  349.9 25.7 %collective-permute-start.31 = (bf16[352,896]{1,0:T(8,128)(2,1)S(1)}, bf16[352,896]{1,0:T(8,128)(2,1)S(1)}, u32[]{:S(2)}, u32[]{:S(2)}) collective-permute-start(bf16[352,896]{1,0:T(8,128)(2,1)S(1)} %get-tuple-element.34), channel_id=1, source_target_pairs={{16,8},{20,12},{24,16},{28,20},{17,9},{21,13},{25,17},{29,21},{18,... | collective-permute-start | bytes 1892360 | tf_op jit(solution)/shard_map/ppermute | solution.py:40
  354.2 34.9 %collective-permute-start.38 = (bf16[352,896]{1,0:T(8,128)(2,1)S(1)}, bf16[352,896]{1,0:T(8,128)(2,1)S(1)}, u32[]{:S(2)}, u32[]{:S(2)}) collective-permute-start(bf16[352,896]{1,0:T(8,128)(2,1)S(1)} %get-tuple-element.38), channel_id=1, source_target_pairs={{16,8},{20,12},{24,16},{28,20},{17,9},{21,13},{25,17},{29,21},{18,... | collective-permute-start | bytes 1892360 | tf_op jit(solution)/shard_map/ppermute | solution.py:40
  362.1 40.6 %collective-permute-start.18 = (bf16[352,896]{1,0:T(8,128)(2,1)S(1)}, bf16[352,896]{1,0:T(8,128)(2,1)S(1)}, u32[]{:S(2)}, u32[]{:S(2)}) collective-permute-start(bf16[352,896]{1,0:T(8,128)(2,1)S(1)} %fusion.44), channel_id=1, source_target_pairs={{8,0},{12,4},{16,8},{20,12},{24,16},{28,20},{9,1},{13,5},{17,9},{2... | collective-permute-start | bytes 1892360 | tf_op jit(solution)/shard_map/ppermute | solution.py:40
  375.6 40.6 %collective-permute-start.25 = (bf16[352,896]{1,0:T(8,128)(2,1)S(1)}, bf16[352,896]{1,0:T(8,128)(2,1)S(1)}, u32[]{:S(2)}, u32[]{:S(2)}) collective-permute-start(bf16[352,896]{1,0:T(8,128)(2,1)S(1)} %fusion.39), channel_id=1, source_target_pairs={{8,0},{12,4},{16,8},{20,12},{24,16},{28,20},{9,1},{13,5},{17,9},{2... | collective-permute-start | bytes 1892360 | tf_op jit(solution)/shard_map/ppermute | solution.py:40
  377.7 38.7 %collective-permute-start.29 = (bf16[352,896]{1,0:T(8,128)(2,1)S(1)}, bf16[352,896]{1,0:T(8,128)(2,1)S(1)}, u32[]{:S(2)}, u32[]{:S(2)}) collective-permute-start(bf16[352,896]{1,0:T(8,128)(2,1)S(1)} %get-tuple-element.33), channel_id=1, source_target_pairs={{0,8},{4,12},{8,16},{12,20},{16,24},{20,28},{1,9},{5,13},{9,17},{1... | collective-permute-start | bytes 1892360 | tf_op jit(solution)/shard_map/ppermute | solution.py:40
  389.2 40.6 %collective-permute-start.32 = (bf16[352,896]{1,0:T(8,128)(2,1)S(1)}, bf16[352,896]{1,0:T(8,128)(2,1)S(1)}, u32[]{:S(2)}, u32[]{:S(2)}) collective-permute-start(bf16[352,896]{1,0:T(8,128)(2,1)S(1)} %fusion.34), channel_id=1, source_target_pairs={{8,0},{12,4},{16,8},{20,12},{24,16},{28,20},{9,1},{13,5},{17,9},{2... | collective-permute-start | bytes 1892360 | tf_op jit(solution)/shard_map/ppermute | solution.py:40
  391.3 38.8 %collective-permute-start.36 = (bf16[352,896]{1,0:T(8,128)(2,1)S(1)}, bf16[352,896]{1,0:T(8,128)(2,1)S(1)}, u32[]{:S(2)}, u32[]{:S(2)}) collective-permute-start(bf16[352,896]{1,0:T(8,128)(2,1)S(1)} %get-tuple-element.37), channel_id=1, source_target_pairs={{0,8},{4,12},{8,16},{12,20},{16,24},{20,28},{1,9},{5,13},{9,17},{1... | collective-permute-start | bytes 1892360 | tf_op jit(solution)/shard_map/ppermute | solution.py:40
  402.7 35.7 %collective-permute-start.39 = (bf16[352,896]{1,0:T(8,128)(2,1)S(1)}, bf16[352,896]{1,0:T(8,128)(2,1)S(1)}, u32[]{:S(2)}, u32[]{:S(2)}) collective-permute-start(bf16[352,896]{1,0:T(8,128)(2,1)S(1)} %fusion.29), channel_id=1, source_target_pairs={{8,0},{12,4},{16,8},{20,12},{24,16},{28,20},{9,1},{13,5},{17,9},{2... | collective-permute-start | bytes 1892360 | tf_op jit(solution)/shard_map/ppermute | solution.py:40
  404.8 11.6 %copy-start.12 = (f32[352,896]{1,0:T(8,128)}, f32[352,896]{1,0:T(8,128)S(1)}, u32[]{:S(2)}) copy-start(f32[352,896]{1,0:T(8,128)S(1)} %fusion.47) | copy-start | bytes 3784708
  416.4 13.5 %copy-start.13 = (f32[352,896]{1,0:T(8,128)}, f32[352,896]{1,0:T(8,128)S(1)}, u32[]{:S(2)}) copy-start(f32[352,896]{1,0:T(8,128)S(1)} %fusion.42) | copy-start | bytes 3784708
  430.1 8.6 %slice-start = ((f32[352,896]{1,0:T(8,128)}), f32[32,896]{1,0:T(8,128)S(1)}, s32[]{:S(2)}) async-start(f32[352,896]{1,0:T(8,128)} %copy-done.12), calls=%async_computation | async-start | bytes 229376 | tf_op jit(solution)/shard_map/slice | solution.py:155
  430.1 8.6 %slice-start.2 = ((f32[352,896]{1,0:T(8,128)}), f32[32,896]{1,0:T(8,128)S(1)}, s32[]{:S(2)}) async-start(f32[352,896]{1,0:T(8,128)} %copy-done.13), calls=%async_computation.2 | async-start | bytes 229376 | tf_op jit(solution)/shard_map/slice | solution.py:155
  430.1 9.4 %slice-start.1 = ((f32[352,896]{1,0:T(8,128)}), f32[320,896]{1,0:T(8,128)S(1)}, s32[]{:S(2)}) async-start(f32[352,896]{1,0:T(8,128)} %copy-done.12), calls=%async_computation.1 | async-start | bytes 2293760 | tf_op jit(solution)/shard_map/slice | solution.py:153
  430.1 9.4 %slice-start.3 = ((f32[352,896]{1,0:T(8,128)}), f32[320,896]{1,0:T(8,128)S(1)}, s32[]{:S(2)}) async-start(f32[352,896]{1,0:T(8,128)} %copy-done.13), calls=%async_computation.3 | async-start | bytes 2293760 | tf_op jit(solution)/shard_map/slice | solution.py:153
  (18 other events, 64.0 us)

commit v2 on v1

--- a/solution.py
+++ b/solution.py
@@ -17,11 +17,17 @@
 
 
 def sum_over(part, axis):
-    distance = 1
-    while distance < lax.axis_size(axis):
+    distance = lax.axis_size(axis) // 2
+    first = None
+    while distance > 0:
         part = part + swap(part, axis, distance)
-        distance *= 2
-    return part
+        first = part if first is None else first
+        distance //= 2
+    return part, first
+
+
+def after(value, *earlier):
+    return lax.optimization_barrier((value,) + earlier)[0]
 
 
 def line_scatter(parts, place, count):
@@ -29,6 +35,7 @@
         return lax.dynamic_index_in_dim(parts, jnp.clip(at, 0, count - 1), 0, keepdims=False)
 
     total = pick(place).astype(F32)
+    firsts = []
     for way in (1, -1):
         moving = None
         for step in range(1, count):
@@ -38,9 +45,11 @@
             froms = range(step) if way == 1 else range(count - step, count)
             route = [(2 * z + x, 2 * (z + way) + x) for z in froms for x in range(2)]
             moving = lax.ppermute(term, "seq", route)
+            if step == 1:
+                firsts.append(moving)
         if moving is not None:
             total = total + moving.astype(F32)
-    return total
+    return total, firsts
 
 
 def forward_body(slots, tile, *refs):
@@ -105,7 +114,6 @@
 def local(tokens, butterfly, low_in, low_out, cotangent):
     rows = tokens.shape[0]
     per_dev, slots, block, hidden = butterfly.shape
-    rank = low_out.shape[0]
     seq = lax.axis_size("seq")
     feat = lax.axis_size("feat")
     local_bits = per_dev.bit_length() - 1
@@ -115,10 +123,11 @@
     side = me % 2
     place = me // 2
     width = block // seq
-    low_width = rank // seq
-
-    low_rank = sum_over(jnp.dot(tokens, low_in, preferred_element_type=F32), "feat").astype(BF16)
-    partners = [swap(tokens, "feat", 1 << r) for r in range(remote)]
+
+    low_rank, first = sum_over(jnp.dot(tokens, low_in, preferred_element_type=F32), "feat")
+    low_rank = low_rank.astype(BF16)
+    leaving = after(tokens, first)
+    partners = [swap(leaving, "feat", 1 << r) for r in reversed(range(remote))][::-1]
 
     def halves(wide, parts):
         return wide.T.reshape(parts, pairs, 2, -1, rows)
@@ -129,55 +138,63 @@
     own_t = halves(tokens, per_dev)
     far_own = swap(side_of(own_t, 1 - side), "seq", 1)
     far = [far_own] + [swap(far_own, "feat", 1 << r) for r in range(remote)]
-    near = [side_of(own_t, side)] + [side_of(halves(p, per_dev), side) for p in partners]
+    activated, grad_pre = forward(tokens, partners, low_rank, butterfly, low_out, cotangent)
+    grads = []
+    for k in range(per_dev):
+        grads.append(jnp.concatenate([grad_pre[k], swap(grad_pre[k], "seq", 1)], axis=0))
+
+    near = [side_of(own_t, side)]
+    near += [side_of(halves(after(p, grad_pre), per_dev), side) for p in partners]
     both = [jnp.concatenate([n, f], axis=-1) for n, f in zip(near, far)]
     rank_t = halves(low_rank, 1)
     both_rank = jnp.concatenate(
         [side_of(rank_t, side), swap(side_of(rank_t, 1 - side), "seq", 1)], axis=-1
     )[0]
 
-    activated, grad_pre = forward(tokens, partners, low_rank, butterfly, low_out, cotangent)
-
-    weight_rows = []
-    for k in range(per_dev):
-        grads = jnp.concatenate([grad_pre[k], swap(grad_pre[k], "seq", 1)], axis=0)
-        picks = [both[0][k]] + [both[0][k ^ 1 << b] for b in range(local_bits)]
-        picks += [both[1 + r][k] for r in range(remote)]
-        left = jnp.concatenate(picks + [both_rank], axis=1)
-        deep = left.shape[1]
-        terms = jnp.dot(
-            left.reshape(pairs * deep, 2 * rows), grads, preferred_element_type=F32
-        ).astype(BF16)
-        weight_rows.append(line_scatter(terms.reshape(pairs, deep, hidden), place, pairs))
-    butterfly_grad = jnp.stack(
-        [w[: slots * width].reshape(slots, width, hidden) for w in weight_rows], axis=0
+    sums = []
+    late = []
+    group = max(1, per_dev // 2)
+    for head in range(0, per_dev, group):
+        terms = []
+        for k in range(head, head + group):
+            picks = [both[0][k]] + [both[0][k ^ 1 << b] for b in range(local_bits)]
+            picks += [both[1 + r][k] for r in range(remote)]
+            left = jnp.concatenate(picks + [both_rank], axis=1)
+            deep = left.shape[1]
+            term = jnp.dot(
+                left.reshape(pairs * deep, 2 * rows), grads[k], preferred_element_type=F32
+            ).astype(BF16)
+            terms.append(term.reshape(pairs, deep, hidden))
+        total, firsts = line_scatter(jnp.stack(terms, axis=1), place, pairs)
+        late += [after(grad_pre[k], *terms, *firsts) for k in range(head, head + group)]
+        sums.append(total)
+    weight_rows = [w[k] for w in sums for k in range(group)]
+    butterfly_grad = jnp.concatenate(
+        [w[:, : slots * width].reshape(group, slots, width, hidden) for w in sums], axis=0
     )
     low_out_grad = jnp.concatenate([w[slots * width :] for w in weight_rows], axis=1)
 
     low_back = sum(
-        dot_t(grad_pre[k], low_out[:, k * hidden : (k + 1) * hidden]) for k in range(per_dev)
-    )
-    low_grad = sum_over(low_back, "feat").astype(BF16)
+        dot_t(late[k], low_out[:, k * hidden : (k + 1) * hidden]) for k in range(per_dev)
+    )
+    low_grad = sum_over(low_back, "feat")[0].astype(BF16)
     in_terms = lax.dot_general(
         low_grad, tokens, (((0,), (0,)), ((), ())), preferred_element_type=F32
-    ).reshape(pairs, 2, low_width, per_dev * block)
-    in_own = lax.dynamic_index_in_dim(in_terms, side, 1, keepdims=False)
-    in_far = lax.dynamic_index_in_dim(in_terms, 1 - side, 1, keepdims=False).astype(BF16)
-    in_pair = (in_own + swap(in_far, "seq", 1).astype(F32)).astype(BF16)
-    low_in_grad = line_scatter(in_pair, place, pairs).T
+    )
+    low_in_grad = lax.psum_scatter(in_terms, "seq", scatter_dimension=0, tiled=True).T
 
     came = []
     for r in range(remote):
         slot = 1 + local_bits + r
-        partial = [dot_t(grad_pre[k], butterfly[k, slot]).astype(BF16) for k in range(per_dev)]
+        partial = [dot_t(late[k], butterfly[k, slot]).astype(BF16) for k in range(per_dev)]
         came.append(swap(jnp.concatenate(partial, axis=1), "feat", 1 << r))
     pieces = []
     for j in range(per_dev):
         at = slice(j * block, (j + 1) * block)
-        total = dot_t(low_grad, low_in[at]) + dot_t(grad_pre[j], butterfly[j, 0])
+        total = dot_t(low_grad, low_in[at]) + dot_t(late[j], butterfly[j, 0])
         for b in range(local_bits):
             i = j ^ 1 << b
-            total = total + dot_t(grad_pre[i], butterfly[i, 1 + b])
+            total = total + dot_t(late[i], butterfly[i, 1 + b])
         for c in came:
             total = total + c[:, at].astype(F32)
         pieces.append(total.astype(BF16))

time: 444 us -> 425 us (0.957)
  waiting for transfers between devices: 214 us -> 178 us
  starting transfers between devices: 75.4 us -> 42.3 us
  matrix products: 67.1 us -> 89.1 us
  other arithmetic: 33 us -> 47.3 us
  between operations: 1.95 us -> 14.9 us
    ppermute x30 -> x12, starting transfers between devices: 60.7 us -> 29.3 us  [line_scatter(): moving = lax.ppermute(term, 'seq', route)]
    ppermute x30 -> x12, waiting for transfers between devices: 121 us -> 93.5 us  [line_scatter(): moving = lax.ppermute(term, 'seq', route)]
    dot_general x28, matrix products: 45.5 us -> 66.1 us  [dot_t(): lax.dot_general(left, right, (((1,), (1,)), ((), ())), preferred_element_...]
    ppermute x17 -> x16, waiting for transfers between devices: 92.3 us -> 84.2 us  [swap(): return lax.ppermute(block, axis, [(i, i ^ distance) for i in range(count)])]
    convert_element_type x15 -> x4, other arithmetic: 8.98 us -> 15.8 us  [line_scatter(): term = (term.astype(F32) + moving.astype(F32)).astype(BF16)]
    unnamed x66 -> x79, local copies, waits for them, and re-layouts: 7.47 us -> 10.9 us
    ppermute x17 -> x16, starting transfers between devices: 14.7 us -> 13 us  [swap(): return lax.ppermute(block, axis, [(i, i ^ distance) for i in range(count)])]
  transfers between devices with their start and end apart: 47 -> 29, of which waited for: 18 -> 15; matrix products, arithmetic and copies ran while one was open for 27% -> 25% of each run, Pallas kernels for 5% -> 5%
where the time goes in v2:
time: 425 us; the launch traced here: 422 us
  waiting for transfers between devices  178 us (42%)
  matrix products  89.1 us (21%)
  other arithmetic  47.3 us (11%)
  starting transfers between devices  42.3 us (10%)
  local copies, waits for them, and re-layouts  29.7 us (7%)
  Pallas kernels  20.8 us (5%)
  between operations  14.9 us (4%)
    ppermute x12, waiting for transfers between devices, line_scatter(): moving = lax.ppermute(term, 'seq', route)  93.5 us
    ppermute x16, waiting for transfers between devices, swap(): return lax.ppermute(block, axis, [(i, i ^ distance) for i in range(count)])  84.2 us
    dot_general x28, matrix products, dot_t(): lax.dot_general(left, right, (((1,), (1,)), ((), ())), preferred_element_...  66.1 us
    ppermute x12, starting transfers between devices, line_scatter(): moving = lax.ppermute(term, 'seq', route)  29.3 us
    pallas_call x1, Pallas kernels, forward(): pl.pallas_call(functools.partial(forward_body, slots, tile), grid=(per_de...  20.8 us
    dot_general x4, matrix products, local(): jnp.dot(left.reshape(pairs * deep, 2 * rows), grads[k], preferred_element...  18.2 us
    convert_element_type x4, other arithmetic, line_scatter(): term = (term.astype(F32) + moving.astype(F32)).astype(BF16)  15.8 us
    ppermute x16, starting transfers between devices, swap(): return lax.ppermute(block, axis, [(i, i ^ distance) for i in range(count)])  13 us
  transfers between devices with their start and end apart: 29, of which 15 were waited for; matrix products, arithmetic and copies ran while one was open for 25% of the time, Pallas kernels for 5%

profile of v2, /device:TPU:16, one launch (start us, length us, event | category | flops | bytes accessed | tf_op | source)
XLA Modules:
  0.0 421.7 jit_solution(9384575354391865869)
XLA Ops:
  7.2 2.7 fusion.169
  11.5 12.1 %collective-permute-done = f32[512,256]{1,0:T(8,128)S(1)} collective-permute-done((f32[512,256]{1,0:T(8,128)S(1)}, f32[512,256]{1,0:T(8,128)S(1)}, u32[]{:S(2)}, u32[]{:S(2)}) %collective-permute-start) | collective-permute-done | bytes 524320 | tf_op jit(solution)/shard_map/ppermute | solution.py:16
  26.1 2.5 copy.20
  28.5 2.7 dynamic-slice_bitcast_fusion.3
  32.7 2.2 collective-permute-done.3
  39.3 18.3 %collective-permute-done.4 = bf16[4,4,64,512]{3,2,1,0:T(8,128)(2,1)} collective-permute-done((bf16[4,4,64,512]{3,2,1,0:T(8,128)(2,1)}, bf16[4,4,64,512]{3,2,1,0:T(8,128)(2,1)}, u32[]{:S(2)}, u32[]{:S(2)}) %collective-permute-start.4) | collective-permute-done | bytes 1048608 | tf_op jit(solution)/shard_map/ppermute | solution.py:16
  63.7 9.4 %collective-permute-done.2.refs_4_ = bf16[512,2048]{1,0:T(8,128)(2,1)} collective-permute-done((bf16[512,2048]{1,0:T(8,128)(2,1)S(1)}, bf16[512,2048]{1,0:T(8,128)(2,1)}, u32[]{:S(2)}, u32[]{:S(2)}) %collective-permute-start.2) | collective-permute-done | bytes 2097184 | tf_op jit(solution)/shard_map/ppermute | solution.py:16
  73.1 20.8 %shard_map.92 = (bf16[512,3584]{1,0:T(8,128)(2,1)}, bf16[4,512,896]{2,1,0:T(8,128)(2,1)}) custom-call(bf16[512,2048]{1,0:T(8,128)(2,1)S(1)} %copy-done, bf16[512,2048]{1,0:T(8,128)(2,1)S(1)} %copy-done, bf16[512,2048]{1,0:T(8,128)(2,1)S(1)} %copy-done, bf16[512,2048]{1,0:T(8,128)(2,1)} %collective-permute-done.1.refs_3_, ...), custom_call_target="tpu_custom_call" | custom-call | flops 10334765056 | bytes 39845888 | tf_op jit(solution)/shard_map/pallas_call | solution.py:86
  93.9 4.0 slice_bitcast_fusion
  99.4 1.9 constant_dynamic-update-slice_fusion.9
  103.9 3.9 copy.21
  107.8 3.9 copy.22
  115.2 2.9 fusion.151
  118.8 2.8 fusion.149
  121.6 2.0 constant_dynamic-update-slice_fusion.12
  123.6 5.6 %convolution_convert_fusion.2 = bf16[1408,896]{1,0:T(8,128)(2,1)S(1)} fusion(bf16[1408,1024]{1,0:T(8,128)(2,1)} %bitcast.306, bf16[512,896]{1,0:T(8,128)(2,1)} %collective-permute-done.9, bf16[512,896]{1,0:T(8,128)(2,1)} %get-tuple-element.20), kind=kOutput, calls=%fused_computation.31 | convolution fusion | flops 2588622848 | bytes 7241728 | tf_op jit(solution)/shard_map/dot_general | solution.py:164
  129.2 11.8 %collective-permute-done.8 = bf16[512,896]{1,0:T(8,128)(2,1)S(1)} collective-permute-done((bf16[512,896]{1,0:T(8,128)(2,1)}, bf16[512,896]{1,0:T(8,128)(2,1)S(1)}, u32[]{:S(2)}, u32[]{:S(2)}) %collective-permute-start.8) | collective-permute-done | bytes 917536 | tf_op jit(solution)/shard_map/ppermute | solution.py:16
  141.1 4.5 %convolution_convert_fusion.3 = bf16[1408,896]{1,0:T(8,128)(2,1)S(1)} fusion(bf16[1408,1024]{1,0:T(8,128)(2,1)S(1)} %bitcast.308, bf16[512,896]{1,0:T(8,128)(2,1)S(1)} %collective-permute-done.8, bf16[512,896]{1,0:T(8,128)(2,1)} %get-tuple-element.19), kind=kOutput, calls=%fused_computation.32 | convolution fusion | flops 2588622848 | bytes 7241728 | tf_op jit(solution)/shard_map/dot_general | solution.py:164
  151.4 9.3 %collective-permute-done.13 = bf16[512,896]{1,0:T(8,128)(2,1)S(1)} collective-permute-done((bf16[512,896]{1,0:T(8,128)(2,1)}, bf16[512,896]{1,0:T(8,128)(2,1)S(1)}, u32[]{:S(2)}, u32[]{:S(2)}) %collective-permute-start.13) | collective-permute-done | bytes 917536 | tf_op jit(solution)/shard_map/ppermute | solution.py:16
  160.7 4.7 %convolution_convert_fusion = bf16[1408,896]{1,0:T(8,128)(2,1)S(1)} fusion(bf16[1408,1024]{1,0:T(8,128)(2,1)S(1)} %bitcast.307, bf16[512,896]{1,0:T(8,128)(2,1)S(1)} %collective-permute-done.13, bf16[512,896]{1,0:T(8,128)(2,1)} %get-tuple-element.22), kind=kOutput, calls=%fused_computation.29 | convolution fusion | flops 2588622848 | bytes 7241728 | tf_op jit(solution)/shard_map/dot_general | solution.py:164
  165.4 13.3 %collective-permute-done.12 = bf16[512,896]{1,0:T(8,128)(2,1)S(1)} collective-permute-done((bf16[512,896]{1,0:T(8,128)(2,1)S(1)}, bf16[512,896]{1,0:T(8,128)(2,1)S(1)}, u32[]{:S(2)}, u32[]{:S(2)}) %collective-permute-start.12) | collective-permute-done | bytes 917536 | tf_op jit(solution)/shard_map/ppermute | solution.py:16
  178.7 3.3 convolution_convert_fusion.1
  182.1 2.0 fusion.47
  187.4 2.2 convolution_convert_fusion.11
  189.6 2.2 convolution_convert_fusion.7
  191.8 24.6 %collective-permute-done.15 = bf16[2,352,896]{2,1,0:T(8,128)(2,1)} collective-permute-done((bf16[2,352,896]{2,1,0:T(8,128)(2,1)}, bf16[2,352,896]{2,1,0:T(8,128)(2,1)}, u32[]{:S(2)}, u32[]{:S(2)}) %collective-permute-start.15) | collective-permute-done | bytes 1261600 | tf_op jit(solution)/shard_map/ppermute | solution.py:47
  216.4 2.2 convolution_convert_fusion.8
  218.6 2.2 convolution_convert_fusion.4
  220.8 2.1 convolution_convert_fusion.9
  222.9 1.9 convolution_convert_fusion.5
  226.9 2.2 convolution_convert_fusion.10
  230.8 3.2 fusion.102
  234.0 2.9 fusion.98
  236.8 3.2 fusion.100
  240.0 3.2 fusion.86
  243.2 3.2 fusion.84
  246.4 3.2 fusion.88
  249.6 3.2 fusion.78
  252.7 3.2 fusion.80
  255.9 3.0 fusion.82
  259.0 3.2 fusion.76
  262.2 3.4 fusion.7
  266.8 4.8 %collective-permute-start.22 = (bf16[2,352,896]{2,1,0:T(8,128)(2,1)}, bf16[2,352,896]{2,1,0:T(8,128)(2,1)}, u32[]{:S(2)}, u32[]{:S(2)}) collective-permute-start(bf16[2,352,896]{2,1,0:T(8,128)(2,1)} %get-tuple-element.38), channel_id=1, source_target_pairs={{16,8},{20,12},{24,16},{28,20},{17,9},{21,13},{25,17},{29,21},{18,... | collective-permute-start | bytes 3784712 | tf_op jit(solution)/shard_map/ppermute | solution.py:47
  276.3 2.2 convolution_convert_fusion.6
  278.5 2.9 fusion.74
  281.5 7.7 %collective-permute-done.16 = f32[512,256]{1,0:T(8,128)S(1)} collective-permute-done((f32[512,256]{1,0:T(8,128)S(1)}, f32[512,256]{1,0:T(8,128)S(1)}, u32[]{:S(2)}, u32[]{:S(2)}) %collective-permute-start.16) | collective-permute-done | bytes 524320 | tf_op jit(solution)/shard_map/ppermute | solution.py:16
  292.3 3.8 fusion.2
  297.4 4.6 %collective-permute-start.26 = (bf16[2,352,896]{2,1,0:T(8,128)(2,1)}, bf16[2,352,896]{2,1,0:T(8,128)(2,1)}, u32[]{:S(2)}, u32[]{:S(2)}) collective-permute-start(bf16[2,352,896]{2,1,0:T(8,128)(2,1)} %get-tuple-element.42), channel_id=1, source_target_pairs={{16,8},{20,12},{24,16},{28,20},{17,9},{21,13},{25,17},{29,21},{18,... | collective-permute-start | bytes 3784712 | tf_op jit(solution)/shard_map/ppermute | solution.py:47
  301.9 2.2 fusion.72
  304.2 2.1 fusion.170
  307.7 4.8 %fusion.8 = (bf16[2,352,896]{2,1,0:T(8,128)(2,1)}, bf16[2,352,896]{2,1,0:T(8,128)(2,1)}) fusion(bf16[2,352,896]{2,1,0:T(8,128)(2,1)S(1)} %copy-done.18, s32[]{:T(128)S(6)} %min.32, bf16[4,1,352,896]{3,2,1,0:T(8,128)(2,1)} %bitcast.289, bf16[4,1,352,896]{3,2,1,0:T(8,128)(2,1)} %bitcast.285, bf16[2,352,896]{2,1,0:T(8,128)(2,1)} %collective-permute-done.22, ...), kind=kLoop, calls=%fused_computation.68 | loop fusion | flops 6307840 | bytes 10092552 | tf_op jit(solution)/shard_map/convert_element_type | solution.py:44
  312.4 2.3 collective-permute-start.21
  314.7 29.8 %collective-permute-done.24 = bf16[2,352,896]{2,1,0:T(8,128)(2,1)} collective-permute-done((bf16[2,352,896]{2,1,0:T(8,128)(2,1)}, bf16[2,352,896]{2,1,0:T(8,128)(2,1)}, u32[]{:S(2)}, u32[]{:S(2)}) %collective-permute-start.24) | collective-permute-done | bytes 1261600 | tf_op jit(solution)/shard_map/ppermute | solution.py:47
  344.6 2.2 collective-permute-start.23
  347.2 3.9 fusion.3
  351.1 4.5 %collective-permute-start.25 = (bf16[2,352,896]{2,1,0:T(8,128)(2,1)}, bf16[2,352,896]{2,1,0:T(8,128)(2,1)}, u32[]{:S(2)}, u32[]{:S(2)}) collective-permute-start(bf16[2,352,896]{2,1,0:T(8,128)(2,1)} %get-tuple-element.39), channel_id=1, source_target_pairs={{0,8},{4,12},{8,16},{12,20},{16,24},{20,28},{1,9},{5,13},{9,17},{1... | collective-permute-start | bytes 3784712 | tf_op jit(solution)/shard_map/ppermute | solution.py:47
  355.7 2.2 collective-permute-start.27
  365.6 2.4 copy.28
  367.9 8.4 %collective-permute-done.21 = bf16[2,352,896]{2,1,0:T(8,128)(2,1)} collective-permute-done((bf16[2,352,896]{2,1,0:T(8,128)(2,1)}, bf16[2,352,896]{2,1,0:T(8,128)(2,1)}, u32[]{:S(2)}, u32[]{:S(2)}) %collective-permute-start.21) | collective-permute-done | bytes 1261600 | tf_op jit(solution)/shard_map/ppermute | solution.py:47
  376.4 8.2 %collective-permute-done.23 = bf16[2,352,896]{2,1,0:T(8,128)(2,1)} collective-permute-done((bf16[2,352,896]{2,1,0:T(8,128)(2,1)}, bf16[2,352,896]{2,1,0:T(8,128)(2,1)}, u32[]{:S(2)}, u32[]{:S(2)}) %collective-permute-start.23) | collective-permute-done | bytes 1261600 | tf_op jit(solution)/shard_map/ppermute | solution.py:47
  384.5 2.6 fusion.9
  387.3 20.1 %collective-permute-done.25 = bf16[2,352,896]{2,1,0:T(8,128)(2,1)} collective-permute-done((bf16[2,352,896]{2,1,0:T(8,128)(2,1)}, bf16[2,352,896]{2,1,0:T(8,128)(2,1)}, u32[]{:S(2)}, u32[]{:S(2)}) %collective-permute-start.25) | collective-permute-done | bytes 1261600 | tf_op jit(solution)/shard_map/ppermute | solution.py:47
  409.3 2.1 fusion.4
  411.6 2.5 pad_maximum_fusion
  (146 shorter events, 59.6 us)
Async XLA Ops:
  7.2 17.4 %copy-start = (bf16[512,2048]{1,0:T(8,128)(2,1)S(1)}, bf16[512,2048]{1,0:T(8,128)(2,1)}, u32[]{:S(2)}) copy-start(bf16[512,2048]{1,0:T(8,128)(2,1)} %refs_2_.1) | copy-start | bytes 6291460
  7.2 407.7 %reduce-scatter.2.cloned.1.call-start = ((), (), s32[]{:S(2)}) async-start(), calls=%async_computation.1 | async-start | bytes 2359296 | tf_op jit(solution)/shard_map/reduce_scatter | solution.py:184
  9.9 13.7 %collective-permute-start = (f32[512,256]{1,0:T(8,128)S(1)}, f32[512,256]{1,0:T(8,128)S(1)}, u32[]{:S(2)}, u32[]{:S(2)}) collective-permute-start(f32[512,256]{1,0:T(8,128)S(1)} %fusion.169), channel_id=1, source_target_pairs={{0,2},{1,3},{2,0},{3,1},{4,6},{5,7},{6,4},{7,5},{8,10},{9,11},{10,... | collective-permute-start | bytes 1572872 | tf_op jit(solution)/shard_map/ppermute | solution.py:16
  24.5 37.5 %collective-permute-start.1 = (bf16[512,2048]{1,0:T(8,128)(2,1)S(1)}, bf16[512,2048]{1,0:T(8,128)(2,1)}, u32[]{:S(2)}, u32[]{:S(2)}) collective-permute-start(bf16[512,2048]{1,0:T(8,128)(2,1)S(1)} %copy-done), channel_id=1, source_target_pairs={{0,1},{1,0},{2,3},{3,2},{4,5},{5,4},{6,7},{7,6},{8,9},{9,8},{10,11... | collective-permute-start | bytes 6291464 | tf_op jit(solution)/shard_map/ppermute | solution.py:16
  24.5 48.5 %collective-permute-start.2 = (bf16[512,2048]{1,0:T(8,128)(2,1)S(1)}, bf16[512,2048]{1,0:T(8,128)(2,1)}, u32[]{:S(2)}, u32[]{:S(2)}) collective-permute-start(bf16[512,2048]{1,0:T(8,128)(2,1)S(1)} %copy-done), channel_id=1, source_target_pairs={{0,2},{1,3},{2,0},{3,1},{4,6},{5,7},{6,4},{7,5},{8,10},{9,11},{10,... | collective-permute-start | bytes 6291464 | tf_op jit(solution)/shard_map/ppermute | solution.py:16
  31.2 26.3 %collective-permute-start.4 = (bf16[4,4,64,512]{3,2,1,0:T(8,128)(2,1)}, bf16[4,4,64,512]{3,2,1,0:T(8,128)(2,1)}, u32[]{:S(2)}, u32[]{:S(2)}) collective-permute-start(bf16[4,4,64,512]{3,2,1,0:T(8,128)(2,1)} %get-tuple-element.72), channel_id=1, source_target_pairs={{0,4},{4,0},{8,12},{12,8},{16,20},{20,16},{24,28},{28,24},{1,5},{5... | collective-permute-start | bytes 3145736 | tf_op jit(solution)/shard_map/ppermute | solution.py:16
  32.7 2.3 collective-permute-start.3
  38.7 82.9 %collective-permute-start.7 = (bf16[1,4,32,512]{3,2,1,0:T(8,128)(2,1)}, bf16[1,4,32,512]{3,2,1,0:T(8,128)(2,1)}, u32[]{:S(2)}, u32[]{:S(2)}) collective-permute-start(bf16[1,4,32,512]{3,2,1,0:T(8,128)(2,1)} %get-tuple-element.80), channel_id=1, source_target_pairs={{0,4},{4,0},{8,12},{12,8},{16,20},{20,16},{24,28},{28,24},{1,5},{5... | collective-permute-start | bytes 393224 | tf_op jit(solution)/shard_map/ppermute | solution.py:16
  57.6 56.0 %collective-permute-start.5 = (bf16[4,4,64,512]{3,2,1,0:T(8,128)(2,1)}, bf16[4,4,64,512]{3,2,1,0:T(8,128)(2,1)}, u32[]{:S(2)}, u32[]{:S(2)}) collective-permute-start(bf16[4,4,64,512]{3,2,1,0:T(8,128)(2,1)} %collective-permute-done.4), channel_id=1, source_target_pairs={{0,1},{1,0},{2,3},{3,2},{4,5},{5,4},{6,7},{7,6},{8,9},{9,8},{10,11... | collective-permute-start | bytes 3145736 | tf_op jit(solution)/shard_map/ppermute | solution.py:16
  57.6 60.6 %collective-permute-start.6 = (bf16[4,4,64,512]{3,2,1,0:T(8,128)(2,1)}, bf16[4,4,64,512]{3,2,1,0:T(8,128)(2,1)}, u32[]{:S(2)}, u32[]{:S(2)}) collective-permute-start(bf16[4,4,64,512]{3,2,1,0:T(8,128)(2,1)} %collective-permute-done.4), channel_id=1, source_target_pairs={{0,2},{1,3},{2,0},{3,1},{4,6},{5,7},{6,4},{7,5},{8,10},{9,11},{10,... | collective-permute-start | bytes 3145736 | tf_op jit(solution)/shard_map/ppermute | solution.py:16
  60.3 12.7 %copy-start.1 = (bf16[256,3584]{1,0:T(8,128)(2,1)S(1)}, bf16[256,3584]{1,0:T(8,128)(2,1)}, u32[]{:S(2)}) copy-start(bf16[256,3584]{1,0:T(8,128)(2,1)} %refs_7_.1) | copy-start | bytes 5505028
  61.9 32.0 %copy-start.32 = (bf16[4,352,1024]{2,1,0:T(8,128)(2,1)}, bf16[4,352,1024]{2,1,0:T(8,128)(2,1)S(1)}, u32[]{:S(2)}) copy-start(bf16[4,352,1024]{2,1,0:T(8,128)(2,1)S(1)} %get-tuple-element.63) | copy-start | bytes 8650756
  62.0 31.9 %copy-start.31 = (bf16[4,352,1024]{2,1,0:T(8,128)(2,1)}, bf16[4,352,1024]{2,1,0:T(8,128)(2,1)S(1)}, u32[]{:S(2)}) copy-start(bf16[4,352,1024]{2,1,0:T(8,128)(2,1)S(1)} %get-tuple-element.74) | copy-start | bytes 8650756
  97.9 25.7 %collective-permute-start.9 = (bf16[512,896]{1,0:T(8,128)(2,1)}, bf16[512,896]{1,0:T(8,128)(2,1)}, u32[]{:S(2)}, u32[]{:S(2)}) collective-permute-start(bf16[512,896]{1,0:T(8,128)(2,1)} %get-tuple-element.20), channel_id=1, source_target_pairs={{0,4},{4,0},{8,12},{12,8},{16,20},{20,16},{24,28},{28,24},{1,5},{5... | collective-permute-start | bytes 2752520 | tf_op jit(solution)/shard_map/ppermute | solution.py:16
  111.7 29.3 %collective-permute-start.8 = (bf16[512,896]{1,0:T(8,128)(2,1)}, bf16[512,896]{1,0:T(8,128)(2,1)S(1)}, u32[]{:S(2)}, u32[]{:S(2)}) collective-permute-start(bf16[512,896]{1,0:T(8,128)(2,1)} %get-tuple-element.19), channel_id=1, source_target_pairs={{0,4},{4,0},{8,12},{12,8},{16,20},{20,16},{24,28},{28,24},{1,5},{5... | collective-permute-start | bytes 2752520 | tf_op jit(solution)/shard_map/ppermute | solution.py:16
  113.6 4.5 %copy-start.15 = (bf16[2048,512]{1,0:T(8,128)(2,1)S(1)}, bf16[2048,512]{1,0:T(8,128)(2,1)}, u32[]{:S(2)}) copy-start(bf16[2048,512]{1,0:T(8,128)(2,1)} %copy.22) | copy-start | bytes 6291460
  113.6 47.1 %collective-permute-start.13 = (bf16[512,896]{1,0:T(8,128)(2,1)}, bf16[512,896]{1,0:T(8,128)(2,1)S(1)}, u32[]{:S(2)}, u32[]{:S(2)}) collective-permute-start(bf16[512,896]{1,0:T(8,128)(2,1)} %get-tuple-element.22), channel_id=1, source_target_pairs={{0,4},{4,0},{8,12},{12,8},{16,20},{20,16},{24,28},{28,24},{1,5},{5... | collective-permute-start | bytes 2752520 | tf_op jit(solution)/shard_map/ppermute | solution.py:16
  115.2 3.0 copy-start.16
  118.2 60.5 %collective-permute-start.12 = (bf16[512,896]{1,0:T(8,128)(2,1)S(1)}, bf16[512,896]{1,0:T(8,128)(2,1)S(1)}, u32[]{:S(2)}, u32[]{:S(2)}) collective-permute-start(bf16[512,896]{1,0:T(8,128)(2,1)S(1)} %copy-done.16), channel_id=1, source_target_pairs={{0,4},{4,0},{8,12},{12,8},{16,20},{20,16},{24,28},{28,24},{1,5},{5... | collective-permute-start | bytes 2752520 | tf_op jit(solution)/shard_map/ppermute | solution.py:16
  123.6 17.4 %copy-start.35 = (bf16[4,352,1024]{2,1,0:T(8,128)(2,1)S(1)}, bf16[4,352,1024]{2,1,0:T(8,128)(2,1)}, u32[]{:S(2)}) copy-start(bf16[4,352,1024]{2,1,0:T(8,128)(2,1)} %get-tuple-element.78) | copy-start | bytes 8650756
  129.2 16.4 %copy-start.3 = (bf16[1408,896]{1,0:T(8,128)(2,1)}, bf16[1408,896]{1,0:T(8,128)(2,1)S(1)}, u32[]{:S(2)}) copy-start(bf16[1408,896]{1,0:T(8,128)(2,1)S(1)} %convolution_convert_fusion.2) | copy-start | bytes 7569412
  145.6 2.6 copy-start.5
  145.6 15.1 %copy-start.33 = (bf16[4,352,1024]{2,1,0:T(8,128)(2,1)S(1)}, bf16[4,352,1024]{2,1,0:T(8,128)(2,1)}, u32[]{:S(2)}) copy-start(bf16[4,352,1024]{2,1,0:T(8,128)(2,1)} %get-tuple-element.75) | copy-start | bytes 8650756
  148.2 39.2 %collective-permute-start.10 = (bf16[2,352,896]{2,1,0:T(8,128)(2,1)}, bf16[2,352,896]{2,1,0:T(8,128)(2,1)}, u32[]{:S(2)}, u32[]{:S(2)}) collective-permute-start(bf16[2,352,896]{2,1,0:T(8,128)(2,1)} %get-tuple-element.46), channel_id=1, source_target_pairs={{0,8},{4,12},{1,9},{5,13},{2,10},{6,14},{3,11},{7,15}} | collective-permute-start | bytes 3784712 | tf_op jit(solution)/shard_map/ppermute | solution.py:47
  150.1 37.3 %collective-permute-start.11 = (bf16[2,352,896]{2,1,0:T(8,128)(2,1)}, bf16[2,352,896]{2,1,0:T(8,128)(2,1)}, u32[]{:S(2)}, u32[]{:S(2)}) collective-permute-start(bf16[2,352,896]{2,1,0:T(8,128)(2,1)} %get-tuple-element.45), channel_id=1, source_target_pairs={{24,16},{28,20},{25,17},{29,21},{26,18},{30,22},{27,19},{31,23}} | collective-permute-start | bytes 3784712 | tf_op jit(solution)/shard_map/ppermute | solution.py:47
  160.7 18.0 %copy-start.37 = (bf16[4,352,1024]{2,1,0:T(8,128)(2,1)S(1)}, bf16[4,352,1024]{2,1,0:T(8,128)(2,1)}, u32[]{:S(2)}) copy-start(bf16[4,352,1024]{2,1,0:T(8,128)(2,1)} %get-tuple-element.77) | copy-start | bytes 8650756
  165.4 16.6 %copy-start.7 = (bf16[1408,896]{1,0:T(8,128)(2,1)}, bf16[1408,896]{1,0:T(8,128)(2,1)S(1)}, u32[]{:S(2)}) copy-start(bf16[1408,896]{1,0:T(8,128)(2,1)S(1)} %convolution_convert_fusion) | copy-start | bytes 7569412
  182.0 2.3 copy-start.11
  184.3 7.5 %collective-permute-start.14 = (bf16[2,352,896]{2,1,0:T(8,128)(2,1)}, bf16[2,352,896]{2,1,0:T(8,128)(2,1)}, u32[]{:S(2)}, u32[]{:S(2)}) collective-permute-start(bf16[2,352,896]{2,1,0:T(8,128)(2,1)} %get-tuple-element.44), channel_id=1, source_target_pairs={{0,8},{4,12},{1,9},{5,13},{2,10},{6,14},{3,11},{7,15}} | collective-permute-start | bytes 3784712 | tf_op jit(solution)/shard_map/ppermute | solution.py:47
  186.0 30.4 %collective-permute-start.15 = (bf16[2,352,896]{2,1,0:T(8,128)(2,1)}, bf16[2,352,896]{2,1,0:T(8,128)(2,1)}, u32[]{:S(2)}, u32[]{:S(2)}) collective-permute-start(bf16[2,352,896]{2,1,0:T(8,128)(2,1)} %get-tuple-element.43), channel_id=1, source_target_pairs={{24,16},{28,20},{25,17},{29,21},{26,18},{30,22},{27,19},{31,23}} | collective-permute-start | bytes 3784712 | tf_op jit(solution)/shard_map/ppermute | solution.py:47
  220.8 4.0 copy-start.2
  255.9 6.3 %copy-start.4 = (bf16[1408,896]{1,0:T(8,128)(2,1)S(1)}, bf16[1408,896]{1,0:T(8,128)(2,1)}, u32[]{:S(2)}) copy-start(bf16[1408,896]{1,0:T(8,128)(2,1)} %copy-done.3) | copy-start | bytes 7569412
  255.9 6.3 %copy-start.6 = (bf16[1408,896]{1,0:T(8,128)(2,1)S(1)}, bf16[1408,896]{1,0:T(8,128)(2,1)}, u32[]{:S(2)}) copy-start(bf16[1408,896]{1,0:T(8,128)(2,1)} %copy-done.5) | copy-start | bytes 7569412
  265.6 31.8 %collective-permute-start.20 = (bf16[2,352,896]{2,1,0:T(8,128)(2,1)S(1)}, bf16[2,352,896]{2,1,0:T(8,128)(2,1)S(1)}, u32[]{:S(2)}, u32[]{:S(2)}) collective-permute-start(bf16[2,352,896]{2,1,0:T(8,128)(2,1)S(1)} %get-tuple-element.37), channel_id=1, source_target_pairs={{0,8},{4,12},{8,16},{12,20},{1,9},{5,13},{9,17},{13,21},{2,10},{6,... | collective-permute-start | bytes 3784712 | tf_op jit(solution)/shard_map/ppermute | solution.py:47
  266.8 39.6 %collective-permute-start.22 = (bf16[2,352,896]{2,1,0:T(8,128)(2,1)}, bf16[2,352,896]{2,1,0:T(8,128)(2,1)}, u32[]{:S(2)}, u32[]{:S(2)}) collective-permute-start(bf16[2,352,896]{2,1,0:T(8,128)(2,1)} %get-tuple-element.38), channel_id=1, source_target_pairs={{16,8},{20,12},{24,16},{28,20},{17,9},{21,13},{25,17},{29,21},{18,... | collective-permute-start | bytes 3784712 | tf_op jit(solution)/shard_map/ppermute | solution.py:47
  273.1 82.5 %collective-permute-start.18 = (bf16[512,2048]{0,1:T(8,128)(2,1)}, bf16[512,2048]{0,1:T(8,128)(2,1)}, u32[]{:S(2)}, u32[]{:S(2)}) collective-permute-start(bf16[512,2048]{0,1:T(8,128)(2,1)} %pad_maximum_fusion.1), channel_id=1, source_target_pairs={{0,1},{1,0},{2,3},{3,2},{4,5},{5,4},{6,7},{7,6},{8,9},{9,8},{10,11... | collective-permute-start | bytes 6291464 | tf_op jit(solution)/shard_map/ppermute | solution.py:16
  274.8 14.4 %collective-permute-start.16 = (f32[512,256]{1,0:T(8,128)S(1)}, f32[512,256]{1,0:T(8,128)S(1)}, u32[]{:S(2)}, u32[]{:S(2)}) collective-permute-start(f32[512,256]{1,0:T(8,128)S(1)} %fusion.71), channel_id=1, source_target_pairs={{0,2},{1,3},{2,0},{3,1},{4,6},{5,7},{6,4},{7,5},{8,10},{9,11},{10,... | collective-permute-start | bytes 1572872 | tf_op jit(solution)/shard_map/ppermute | solution.py:16
  281.5 10.8 %copy-start.8 = (bf16[1408,896]{1,0:T(8,128)(2,1)S(1)}, bf16[1408,896]{1,0:T(8,128)(2,1)}, u32[]{:S(2)}) copy-start(bf16[1408,896]{1,0:T(8,128)(2,1)} %copy-done.7) | copy-start | bytes 7569412
  281.5 10.8 %copy-start.12 = (bf16[1408,896]{1,0:T(8,128)(2,1)S(1)}, bf16[1408,896]{1,0:T(8,128)(2,1)}, u32[]{:S(2)}) copy-start(bf16[1408,896]{1,0:T(8,128)(2,1)} %copy-done.11) | copy-start | bytes 7569412
  289.2 6.8 %collective-permute-start.17 = (f32[512,256]{1,0:T(8,128)S(1)}, f32[512,256]{1,0:T(8,128)S(1)}, u32[]{:S(2)}, u32[]{:S(2)}) collective-permute-start(f32[512,256]{1,0:T(8,128)S(1)} %add.186), channel_id=1, source_target_pairs={{0,1},{1,0},{2,3},{3,2},{4,5},{5,4},{6,7},{7,6},{8,9},{9,8},{10,11... | collective-permute-start | bytes 1572872 | tf_op jit(solution)/shard_map/ppermute | solution.py:16
  290.8 67.1 %collective-permute-start.19 = (bf16[512,2048]{0,1:T(8,128)(2,1)}, bf16[512,2048]{0,1:T(8,128)(2,1)}, u32[]{:S(2)}, u32[]{:S(2)}) collective-permute-start(bf16[512,2048]{0,1:T(8,128)(2,1)} %pad_maximum_fusion.2), channel_id=1, source_target_pairs={{0,2},{1,3},{2,0},{3,1},{4,6},{5,7},{6,4},{7,5},{8,10},{9,11},{10,... | collective-permute-start | bytes 6291464 | tf_op jit(solution)/shard_map/ppermute | solution.py:16
  296.1 48.5 %collective-permute-start.24 = (bf16[2,352,896]{2,1,0:T(8,128)(2,1)}, bf16[2,352,896]{2,1,0:T(8,128)(2,1)}, u32[]{:S(2)}, u32[]{:S(2)}) collective-permute-start(bf16[2,352,896]{2,1,0:T(8,128)(2,1)} %get-tuple-element.41), channel_id=1, source_target_pairs={{0,8},{4,12},{8,16},{12,20},{1,9},{5,13},{9,17},{13,21},{2,10},{6,... | collective-permute-start | bytes 3784712 | tf_op jit(solution)/shard_map/ppermute | solution.py:47
  297.4 6.9 %copy-start.17 = (bf16[2,352,896]{2,1,0:T(8,128)(2,1)}, bf16[2,352,896]{2,1,0:T(8,128)(2,1)S(1)}, u32[]{:S(2)}) copy-start(bf16[2,352,896]{2,1,0:T(8,128)(2,1)S(1)} %collective-permute-done.20) | copy-start | bytes 3784708
  297.4 49.8 %collective-permute-start.26 = (bf16[2,352,896]{2,1,0:T(8,128)(2,1)}, bf16[2,352,896]{2,1,0:T(8,128)(2,1)}, u32[]{:S(2)}, u32[]{:S(2)}) collective-permute-start(bf16[2,352,896]{2,1,0:T(8,128)(2,1)} %get-tuple-element.42), channel_id=1, source_target_pairs={{16,8},{20,12},{24,16},{28,20},{17,9},{21,13},{25,17},{29,21},{18,... | collective-permute-start | bytes 3784712 | tf_op jit(solution)/shard_map/ppermute | solution.py:47
  306.4 40.8 %copy-start.9 = (bf16[1408,896]{1,0:T(8,128)(2,1)S(1)}, bf16[1408,896]{1,0:T(8,128)(2,1)}, u32[]{:S(2)}) copy-start(bf16[1408,896]{1,0:T(8,128)(2,1)} %copy-done.7) | copy-start | bytes 7569412
  306.4 40.8 %copy-start.13 = (bf16[1408,896]{1,0:T(8,128)(2,1)S(1)}, bf16[1408,896]{1,0:T(8,128)(2,1)}, u32[]{:S(2)}) copy-start(bf16[1408,896]{1,0:T(8,128)(2,1)} %copy-done.11) | copy-start | bytes 7569412
  312.4 63.9 %collective-permute-start.21 = (bf16[2,352,896]{2,1,0:T(8,128)(2,1)}, bf16[2,352,896]{2,1,0:T(8,128)(2,1)}, u32[]{:S(2)}, u32[]{:S(2)}) collective-permute-start(bf16[2,352,896]{2,1,0:T(8,128)(2,1)} %get-tuple-element.35), channel_id=1, source_target_pairs={{0,8},{4,12},{8,16},{12,20},{16,24},{20,28},{1,9},{5,13},{9,17},{1... | collective-permute-start | bytes 3784712 | tf_op jit(solution)/shard_map/ppermute | solution.py:47
  344.6 13.3 %copy-start.19 = (bf16[2048,256]{1,0:T(8,128)(2,1)S(1)}, bf16[2048,256]{1,0:T(8,128)(2,1)}, u32[]{:S(2)}) copy-start(bf16[2048,256]{1,0:T(8,128)(2,1)} %param.7) | copy-start | bytes 3145732
  344.6 13.3 %copy-start.27 = (f32[512,512]{0,1:T(8,128)S(1)}, f32[512,512]{0,1:T(8,128)}, u32[]{:S(2)}) copy-start(f32[512,512]{0,1:T(8,128)} %fusion.102) | copy-start | bytes 3145732
  344.6 13.3 %copy-start.28 = (f32[512,512]{0,1:T(8,128)S(1)}, f32[512,512]{0,1:T(8,128)}, u32[]{:S(2)}) copy-start(f32[512,512]{0,1:T(8,128)} %fusion.98) | copy-start | bytes 3145732
  344.6 13.3 %copy-start.29 = (f32[512,512]{0,1:T(8,128)S(1)}, f32[512,512]{0,1:T(8,128)}, u32[]{:S(2)}) copy-start(f32[512,512]{0,1:T(8,128)} %fusion.100) | copy-start | bytes 3145732
  344.6 40.0 %collective-permute-start.23 = (bf16[2,352,896]{2,1,0:T(8,128)(2,1)}, bf16[2,352,896]{2,1,0:T(8,128)(2,1)}, u32[]{:S(2)}, u32[]{:S(2)}) collective-permute-start(bf16[2,352,896]{2,1,0:T(8,128)(2,1)} %get-tuple-element.36), channel_id=1, source_target_pairs={{8,0},{12,4},{16,8},{20,12},{24,16},{28,20},{9,1},{13,5},{17,9},{2... | collective-permute-start | bytes 3784712 | tf_op jit(solution)/shard_map/ppermute | solution.py:47
  351.1 56.4 %collective-permute-start.25 = (bf16[2,352,896]{2,1,0:T(8,128)(2,1)}, bf16[2,352,896]{2,1,0:T(8,128)(2,1)}, u32[]{:S(2)}, u32[]{:S(2)}) collective-permute-start(bf16[2,352,896]{2,1,0:T(8,128)(2,1)} %get-tuple-element.39), channel_id=1, source_target_pairs={{0,8},{4,12},{8,16},{12,20},{16,24},{20,28},{1,9},{5,13},{9,17},{1... | collective-permute-start | bytes 3784712 | tf_op jit(solution)/shard_map/ppermute | solution.py:47
  355.6 3.9 copy-start.24
  355.6 3.9 copy-start.25
  355.7 3.9 copy-start.26
  355.7 53.7 %collective-permute-start.27 = (bf16[2,352,896]{2,1,0:T(8,128)(2,1)}, bf16[2,352,896]{2,1,0:T(8,128)(2,1)}, u32[]{:S(2)}, u32[]{:S(2)}) collective-permute-start(bf16[2,352,896]{2,1,0:T(8,128)(2,1)} %get-tuple-element.40), channel_id=1, source_target_pairs={{8,0},{12,4},{16,8},{20,12},{24,16},{28,20},{9,1},{13,5},{17,9},{2... | collective-permute-start | bytes 3784712 | tf_op jit(solution)/shard_map/ppermute | solution.py:47
  359.6 1.9 copy-start.21
  359.6 1.9 copy-start.22
  359.6 2.2 copy-start.23
  361.8 1.9 copy-start.20
  361.8 1.9 copy-start.30
  384.5 24.8 %copy-start.14 = (bf16[1408,896]{1,0:T(8,128)(2,1)S(1)}, bf16[1408,896]{1,0:T(8,128)(2,1)}, u32[]{:S(2)}) copy-start(bf16[1408,896]{1,0:T(8,128)(2,1)} %copy-done.11) | copy-start | bytes 7569412
  387.2 22.2 %copy-start.10 = (bf16[1408,896]{1,0:T(8,128)(2,1)S(1)}, bf16[1408,896]{1,0:T(8,128)(2,1)}, u32[]{:S(2)}) copy-start(bf16[1408,896]{1,0:T(8,128)(2,1)} %copy-done.7) | copy-start | bytes 7569412
  (3 other events, 4.6 us)
Sparse Core Ops, SparseCore 0:
  306.5 82.0 reduce-scatter.1
